TPU v7x, 32 devices: a whole 2x2x4 slice. The times are simulated.
32 devices in a mesh: gy: 2 (over y), gx: 4 (over x, core), dp: 4 (over z).
Axes of the slice: x: 2, y: 2, z: 4, core: 2. Of those that a mesh axis runs over, the one named last changes fastest.
Arguments:
- features: bfloat16 [4, 32, 64, 512], P('dp', 'gy', 'gx'), may hold values from -36 to 36
- gain_first: float32 [512], replicated, may hold values from 0.1 to 1.9
- gain_second: float32 [512], replicated, may hold values from 0.1 to 1.9
- kernel: float32 [31, 31, 512], replicated, may hold values from -0.1875 to 0.1875
- up_weight: bfloat16 [512, 2048], replicated, may hold values from -0.25 to 0.25
- down_weight: bfloat16 [2048, 512], replicated, may hold values from -0.125 to 0.125
- cotangent: bfloat16 [4, 32, 64, 512], P('dp', 'gy', 'gx'), may hold values from -20 to 20
Outputs:
- grad_input: bfloat16 [4, 32, 64, 512], P('dp', 'gy', 'gx')
- grad_up: float32 [2048, 512], P(('gy', 'gx', 'dp'))
- grad_down: float32 [2048, 512], P(('gy', 'gx', 'dp'))
- grad_kernel: float32 [31, 31, 512], replicated
- grad_gain_first: float32 [512], replicated
- grad_gain_second: float32 [512], replicated
All inputs are finite; a program needn't handle non-finite values.
Results may differ from a plain program's by a relative error of at most 0.0058.
Values may be sent and summed in bfloat16 or wider, within the bound.
A program may use at most 128 MiB of HBM per device.

v0:
```python
import jax
import jax.numpy as jnp
from jax import lax
from jax.sharding import PartitionSpec as P

EPS = 1e-06
GELU_C = 0.7978845608028654
GELU_A = 0.044715


def padded_2(x, sides, width):
    for axis, dim in sides:
        size, length = (lax.axis_size(axis), x.shape[dim])
        up = [(i, (i + 1) % size) for i in range(size - 1)]
        down = [(j, i) for i, j in up]
        last = lax.slice_in_dim(x, length - width, length, axis=dim)
        initial = lax.slice_in_dim(x, 0, width, axis=dim)
        before = lax.ppermute(last, axis, up)
        after = lax.ppermute(initial, axis, down)
        x = jnp.concatenate([before, x, after], axis=dim)
    return x


def gelu_parts(hidden):
    tangent = jnp.tanh(GELU_C * (hidden + GELU_A * hidden * hidden * hidden))
    value = 0.5 * hidden * (1.0 + tangent)
    slope = 0.5 * (1.0 + tangent) + 0.5 * hidden * (1.0 - tangent * tangent) * GELU_C * (
        1.0 + 3.0 * GELU_A * hidden * hidden
    )
    return (value, slope)


def norm_forward(source, gain):
    mean_val = jnp.mean(source, axis=-1, keepdims=True)
    centred = source - mean_val
    spread = jnp.mean(centred * centred, axis=-1, keepdims=True)
    scale_inv = lax.rsqrt(spread + EPS)
    normed = centred * scale_inv
    return (normed * gain, normed, scale_inv)


def norm_backward(upstream, gain, normed, scale_inv):
    scaled = upstream * gain
    return scale_inv * (
        scaled
        - jnp.mean(scaled, axis=-1, keepdims=True)
        - normed * jnp.mean(scaled * normed, axis=-1, keepdims=True)
    )


def extend(source, reach):
    return padded_2(source, (("gy", 1), ("gx", 2)), reach)


def slide(padded, taps, tile_rows, tile_cols):
    side = taps.shape[0]
    start_total = jnp.zeros((padded.shape[0], tile_rows, tile_cols, padded.shape[3]), jnp.float32)

    def slide_one_row(tap_row, totals):
        strip_rows = lax.dynamic_slice_in_dim(padded, tap_row, tile_rows, 1)
        weights_row = lax.dynamic_index_in_dim(taps, tap_row, 0, keepdims=False)
        for tap_col in range(side):
            totals = (
                totals + strip_rows[:, :, tap_col : tap_col + tile_cols, :] * weights_row[tap_col]
            )
        return totals

    return lax.fori_loop(0, side, slide_one_row, start_total)


def tap_sums(padded, grad_conv, side, tile_rows, tile_cols):
    grad_wide = grad_conv.astype(jnp.float32)

    def tap_one_row(tap_row):
        strip_rows = lax.dynamic_slice_in_dim(padded, tap_row, tile_rows, 1)
        return jnp.stack(
            [
                jnp.sum(
                    strip_rows[:, :, tap_col : tap_col + tile_cols, :].astype(jnp.float32)
                    * grad_wide,
                    axis=(0, 1, 2),
                )
                for tap_col in range(side)
            ]
        )

    return lax.map(tap_one_row, jnp.arange(side, dtype=jnp.int32))


def local(features, gain_first, gain_second, kernel, up_weight, down_weight, cotangent):
    channels = features.shape[3]
    tile_rows = features.shape[1]
    tile_cols = features.shape[2]
    side = kernel.shape[0]
    reach = side // 2
    inputs = features.astype(jnp.float32)
    first, normed_first, inv_first = norm_forward(inputs, gain_first)
    conv_in = first.astype(jnp.bfloat16)
    padded_in = extend(conv_in, reach)
    conv_out = slide(padded_in, kernel, tile_rows, tile_cols)
    mixed = inputs + conv_out
    second, normed_second, inv_second = norm_forward(mixed, gain_second)
    mlp_in = second.astype(jnp.bfloat16).reshape(-1, channels)
    hidden = jnp.dot(mlp_in, up_weight, preferred_element_type=jnp.float32)
    value, slope = gelu_parts(hidden)
    activated = value.astype(jnp.bfloat16)
    upstream = cotangent.reshape(-1, channels)
    grad_act = lax.dot_general(
        upstream, down_weight, (((1,), (1,)), ((), ())), preferred_element_type=jnp.float32
    )
    grad_hidden = (grad_act * slope).astype(jnp.bfloat16)
    up_rows = lax.dot_general(
        grad_hidden, mlp_in, (((0,), (0,)), ((), ())), preferred_element_type=jnp.float32
    )
    down_rows = lax.dot_general(
        activated, upstream, (((0,), (0,)), ((), ())), preferred_element_type=jnp.float32
    )
    summed = lax.psum_scatter(
        jnp.concatenate([up_rows, down_rows], axis=1),
        ("gy", "gx", "dp"),
        scatter_dimension=0,
        tiled=True,
    )
    grad_normed = lax.dot_general(
        grad_hidden, up_weight, (((1,), (1,)), ((), ())), preferred_element_type=jnp.float32
    ).reshape(mixed.shape)
    grad_mixed = cotangent.astype(jnp.float32) + norm_backward(
        grad_normed, gain_second, normed_second, inv_second
    )
    grad_conv = grad_mixed.astype(jnp.bfloat16)
    padded_grad = extend(grad_conv, reach)
    grad_source = slide(padded_grad, kernel[::-1, ::-1], tile_rows, tile_cols)
    grad_taps = tap_sums(padded_in, grad_conv, side, tile_rows, tile_cols)
    grad_input = (
        grad_mixed + norm_backward(grad_source, gain_first, normed_first, inv_first)
    ).astype(jnp.bfloat16)
    small_sums = lax.psum(
        (
            grad_taps,
            jnp.sum(grad_source * normed_first, axis=(0, 1, 2)),
            jnp.sum(grad_normed * normed_second, axis=(0, 1, 2)),
        ),
        ("gy", "gx", "dp"),
    )
    divisor = tile_rows * lax.axis_size("gy")
    return (
        grad_input,
        summed[:, :channels] / divisor,
        summed[:, channels:] / divisor,
        small_sums[0] / divisor,
        small_sums[1] / divisor,
        small_sums[2] / divisor,
    )


def solution(mesh):
    in_specs = (P("dp", "gy", "gx", None), P(), P(), P(), P(), P(), P("dp", "gy", "gx", None))
    out_specs = (
        P("dp", "gy", "gx", None),
        P(("gy", "gx", "dp"), None),
        P(("gy", "gx", "dp"), None),
        P(),
        P(),
        P(),
    )
    return jax.shard_map(local, mesh=mesh, in_specs=in_specs, out_specs=out_specs, check_vma=False)
```

profile of v0, /device:TPU:0, one launch (start us, length us, event | category | flops | bytes accessed | tf_op | source)
XLA Modules:
  0.0 1324.0 jit_solution(10352521207322974554)
XLA Ops:
  43.2 412.2 %while.39 = (s32[]{:T(128)}, f32[1,16,16,512]{3,2,1,0:T(8,128)S(1)}, bf16[1,46,46,512]{3,2,1,0:T(8,128)(2,1)}, f32[31,31,512]{2,1,0:T(8,128)}, s32[]{:T(128)}, /...) while((s32[]{:T(128)}, ...), condition=%wide.region_3.4_spmd.clone, body=%wide.region_2.3_spmd.clone.sunk | while | flops 12320801 | bytes 9366443 | solution.py:68
  135.4 11.4 multiply_add_fusion.6
  175.4 11.3 multiply_add_fusion.6
  333.3 11.6 multiply_add_fusion.6
  373.8 12.0 multiply_add_fusion.6
  388.0 11.6 multiply_add_fusion.6
  401.9 12.0 multiply_add_fusion.6
  416.3 11.8 multiply_add_fusion.6
  430.2 11.6 multiply_add_fusion.6
  465.3 344.3 %while.38 = (s32[]{:T(128)}, f32[31,31,512]{2,1,0:T(8,128)}, s32[31]{0:T(128)S(1)}, bf16[1,46,46,512]{3,2,1,0:T(8,128)(2,1)}, f32[1,16,16,512]{3,2,1,0:T(8,128)S...) while((s32[]{:T(128)}, f32[31,31,512]{2,1,0:T(8,128)}, ...), condition=%wide.region_45.46_spmd, body=%wide.region_13.45_spmd.sunk | while | flops 12173859 | bytes 18162564 | solution.py:87
  852.3 415.2 %while.40 = (s32[]{:T(128)}, f32[1,16,16,512]{3,2,1,0:T(8,128)S(1)}, bf16[1,46,46,512]{3,2,1,0:T(8,128)(2,1)}, f32[31,31,512]{2,1,0:T(8,128)}, s32[]{:T(128)}, /...) while((s32[]{:T(128)}, ...), condition=%wide.region_9.10_spmd.clone, body=%wide.region_8.9_spmd.clone.sunk | while | flops 12320801 | bytes 9366443 | solution.py:68
  881.4 11.5 multiply_add_fusion.7
  934.1 11.4 multiply_add_fusion.7
  961.1 11.3 multiply_add_fusion.7
  974.7 11.5 multiply_add_fusion.7
  988.5 11.8 multiply_add_fusion.7
  1002.5 11.4 multiply_add_fusion.7
  1016.1 11.4 multiply_add_fusion.7
  1029.7 11.4 multiply_add_fusion.7
  1213.6 11.6 multiply_add_fusion.7
  1227.5 11.6 multiply_add_fusion.7
  1241.3 12.4 multiply_add_fusion.7
  1255.9 11.6 multiply_add_fusion.7
  1267.9 41.4 %all-reduce = (f32[512]{0:T(512)S(1)}, f32[512]{0:T(512)S(1)}) all-reduce(f32[512]{0:T(512)S(1)} %get-tuple-element.286, f32[512]{0:T(512)S(1)} %get-tuple-element.288), channel_id=1, replica_groups=mesh['gy'=2,'gx'=4,'dp'=4] {'gy','gx','dp'}, use_global_device_ids=true, to_apply=%region_48.49 | all-reduce | flops 1024 | bytes 8192 | tf_op jit(solution)/shard_map/psum | solution.py:137
  (514 shorter events, 973.4 us)
Async XLA Ops:
  7.2 449.3 %copy-start = (bf16[512,2048]{1,0:T(8,128)(2,1)S(1)}, bf16[512,2048]{1,0:T(8,128)(2,1)}, u32[]{:S(2)}) copy-start(bf16[512,2048]{1,0:T(8,128)(2,1)} %param.17) | copy-start | bytes 6291460
  7.2 1303.8 %all-reduce.3.cloned.1.call-start = ((), (), s32[]{:S(2)}) async-start(), calls=%async_computation.1 | async-start | bytes 4063232 | tf_op jit(solution)/shard_map/psum | solution.py:137
  10.8 10.1 collective-permute-start
  15.7 9.3 collective-permute-start.1
  27.5 10.4 collective-permute-start.3
  30.1 9.4 collective-permute-start.2
  43.2 412.2 %copy-start.7 = (bf16[1,16,16,512]{3,2,1,0:T(8,128)(2,1)S(1)}, bf16[1,16,16,512]{3,2,1,0:T(8,128)(2,1)}, u32[]{:S(2)}) copy-start(bf16[1,16,16,512]{3,2,1,0:T(8,128)(2,1)} %param.13) | copy-start | bytes 786436
  43.2 413.1 %copy-start.25 = (f32[512]{0:T(512)S(1)}, f32[512]{0:T(512)}, u32[]{:S(2)}) copy-start(f32[512]{0:T(512)} %param.15) | copy-start | bytes 6148
  490.1 6.1 copy-start.2
  501.5 6.3 copy-start.2
  524.4 6.1 copy-start.2
  558.1 6.1 copy-start.2
  809.6 504.7 %reduce-scatter.4.cloned.1.call-start = ((), (), s32[]{:S(2)}) async-start(), calls=%async_computation.2 | async-start | bytes 8650752
  810.9 5.2 collective-permute-start.4
  812.4 9.2 copy-start.9
  812.4 8.5 collective-permute-start.5
  822.0 10.9 copy-start.12
  822.0 10.9 copy-start.16
  824.6 22.2 %collective-permute-start.7 = (bf16[1,46,15,512]{3,1,2,0:T(8,128)(2,1)}, bf16[1,46,15,512]{3,1,2,0:T(8,128)(2,1)}, u32[]{:S(2)}, u32[]{:S(2)}) collective-permute-start(bf16[1,46,15,512]{3,1,2,0:T(8,128)(2,1)} %copy.34), channel_id=1, source_target_pairs={{4,0},{8,4},{12,8},{5,1},{9,5},{13,9},{6,2},{10,6},{14,10},{7,3},{... | collective-permute-start | bytes 2119688 | tf_op jit(solution)/shard_map/ppermute | solution.py:19
  825.9 22.5 %collective-permute-start.6 = (bf16[1,46,15,512]{3,1,2,0:T(8,128)(2,1)}, bf16[1,46,15,512]{3,1,2,0:T(8,128)(2,1)}, u32[]{:S(2)}, u32[]{:S(2)}) collective-permute-start(bf16[1,46,15,512]{3,1,2,0:T(8,128)(2,1)} %copy.33), channel_id=1, source_target_pairs={{0,4},{4,8},{8,12},{1,5},{5,9},{9,13},{2,6},{6,10},{10,14},{3,7},{... | collective-permute-start | bytes 2119688 | tf_op jit(solution)/shard_map/ppermute | solution.py:18
  852.3 415.2 %copy-start.26 = (f32[512]{0:T(512)S(1)}, f32[512]{0:T(512)}, u32[]{:S(2)}) copy-start(f32[512]{0:T(512)} %param.14) | copy-start | bytes 6148
  852.3 457.6 %copy-start.8 = (f32[256,512]{1,0:T(8,128)S(1)}, f32[256,512]{1,0:T(8,128)}, u32[]{:S(2)}) copy-start(f32[256,512]{1,0:T(8,128)} %get-tuple-element.396) | copy-start | bytes 1572868
  852.3 457.6 %copy-start.14 = (bf16[1,16,16,512]{3,2,1,0:T(8,128)(2,1)S(1)}, bf16[1,16,16,512]{3,2,1,0:T(8,128)(2,1)}, u32[]{:S(2)}) copy-start(bf16[1,16,16,512]{3,2,1,0:T(8,128)(2,1)} %param.19) | copy-start | bytes 786436
  1310.9 6.2 copy-start.1
  (44 other events, 194.8 us)
Sparse Core Ops, SparseCore 0:
  809.8 137.8 all-reduce.2
  950.1 185.1 reduce-scatter.3
where the time goes:
time: 1340 us; the launch traced here: 1320 us
  other arithmetic  951 us (71%)
  local copies, waits for them, and re-layouts  212 us (16%)
  loops' own time  62.6 us (5%)
  blocking collectives  41.4 us (3%)
  starting transfers between devices  22.6 us (2%)
  between operations  14.6 us (1%)
    add x62, other arithmetic, slide_one_row(): totals + strip_rows[:, :, tap_col:tap_col + tile_cols, :] * weights_row[t...  689 us
    reduce_sum x62, other arithmetic, tap_one_row(): jnp.sum(strip_rows[:, :, tap_col:tap_col + tile_cols, :].astype(jnp.float...  241 us
    slice x124, local copies, waits for them, and re-layouts, slide_one_row(): weights_row[tap_col]  137 us
    another operation x1, loops' own time, tap_sums(): return lax.map(tap_one_row, jnp.arange(side, dtype=jnp.int32))  60.9 us
    psum x1, blocking collectives, local(): lax.psum((grad_taps, jnp.sum(grad_source * normed_first, axis=(0, 1, 2)),...  41.4 us
  transfers between devices with their start and end apart: 10, of which 4 were waited for; matrix products, arithmetic and copies ran while one was open for 34% of the time, Pallas kernels for 0%

commit v1 on v0

--- a/solution.py
+++ b/solution.py
@@ -1,5 +1,6 @@
 import jax
 import jax.numpy as jnp
+import numpy as np
 from jax import lax
 from jax.sharding import PartitionSpec as P
 
@@ -52,39 +53,45 @@
     return padded_2(source, (("gy", 1), ("gx", 2)), reach)
 
 
-def slide(padded, taps, tile_rows, tile_cols):
-    side = taps.shape[0]
-    start_total = jnp.zeros((padded.shape[0], tile_rows, tile_cols, padded.shape[3]), jnp.float32)
+def transform_tables(tile_rows, tile_cols, side):
+    rows, cols = tile_rows + side - 1, tile_cols + side - 1
+    freqs, weight = [], []
+    for fx in range(cols // 2 + 1):
+        self_paired = 2 * fx % cols == 0
+        for fy in range(rows // 2 + 1 if self_paired else rows):
+            freqs.append((fy, fx))
+            alone = self_paired and 2 * fy % rows == 0
+            weight.append((1.0 if alone else 2.0) / (rows * cols))
+    freqs = np.array(freqs)
 
-    def slide_one_row(tap_row, totals):
-        strip_rows = lax.dynamic_slice_in_dim(padded, tap_row, tile_rows, 1)
-        weights_row = lax.dynamic_index_in_dim(taps, tap_row, 0, keepdims=False)
-        for tap_col in range(side):
-            totals = (
-                totals + strip_rows[:, :, tap_col : tap_col + tile_cols, :] * weights_row[tap_col]
-            )
-        return totals
+    def table(row_ids, col_ids):
+        angle = 2 * np.pi * (
+            (freqs[:, :1] * row_ids % rows)[:, :, None] / rows
+            + (freqs[:, 1:] * col_ids % cols)[:, None, :] / cols
+        )
+        angle = angle.reshape(len(freqs), -1)
+        return jnp.asarray(np.concatenate([np.cos(angle), -np.sin(angle)]), jnp.bfloat16)
 
-    return lax.fori_loop(0, side, slide_one_row, start_total)
+    whole = table(np.arange(rows), np.arange(cols))
+    corner = table(np.arange(tile_rows), np.arange(tile_cols))
+    shifted = table(np.arange(tile_rows) + side - 1, np.arange(tile_cols) + side - 1)
+    taps = table(np.arange(side), np.arange(side))
+    return whole, corner, shifted, taps, np.array(weight, np.float32)[:, None]
 
 
-def tap_sums(padded, grad_conv, side, tile_rows, tile_cols):
-    grad_wide = grad_conv.astype(jnp.float32)
+def forward_transform(table, values):
+    out = jnp.einsum("fp,bpc->bfc", table, values, preferred_element_type=jnp.float32)
+    count = table.shape[0] // 2
+    return out[:, :count], out[:, count:]
 
-    def tap_one_row(tap_row):
-        strip_rows = lax.dynamic_slice_in_dim(padded, tap_row, tile_rows, 1)
-        return jnp.stack(
-            [
-                jnp.sum(
-                    strip_rows[:, :, tap_col : tap_col + tile_cols, :].astype(jnp.float32)
-                    * grad_wide,
-                    axis=(0, 1, 2),
-                )
-                for tap_col in range(side)
-            ]
-        )
 
-    return lax.map(tap_one_row, jnp.arange(side, dtype=jnp.int32))
+def inverse_transform(table, real, imag):
+    spectrum = jnp.concatenate([real, imag], axis=1).astype(jnp.bfloat16)
+    return jnp.einsum("fp,bfc->bpc", table, spectrum, preferred_element_type=jnp.float32)
+
+
+def flat(values):
+    return values.reshape(values.shape[0], -1, values.shape[3])
 
 
 def local(features, gain_first, gain_second, kernel, up_weight, down_weight, cotangent):
@@ -97,7 +104,16 @@
     first, normed_first, inv_first = norm_forward(inputs, gain_first)
     conv_in = first.astype(jnp.bfloat16)
     padded_in = extend(conv_in, reach)
-    conv_out = slide(padded_in, kernel, tile_rows, tile_cols)
+    whole, corner, shifted, tap_table, weight = transform_tables(tile_rows, tile_cols, side)
+    kernel_real, kernel_imag = forward_transform(
+        tap_table, kernel.reshape(1, side * side, channels).astype(jnp.bfloat16)
+    )
+    in_real, in_imag = forward_transform(whole, flat(padded_in))
+    conv_out = inverse_transform(
+        corner,
+        weight * (in_real * kernel_real + in_imag * kernel_imag),
+        weight * (in_imag * kernel_real - in_real * kernel_imag),
+    ).reshape(inputs.shape)
     mixed = inputs + conv_out
     second, normed_second, inv_second = norm_forward(mixed, gain_second)
     mlp_in = second.astype(jnp.bfloat16).reshape(-1, channels)
@@ -129,8 +145,18 @@
     )
     grad_conv = grad_mixed.astype(jnp.bfloat16)
     padded_grad = extend(grad_conv, reach)
-    grad_source = slide(padded_grad, kernel[::-1, ::-1], tile_rows, tile_cols)
-    grad_taps = tap_sums(padded_in, grad_conv, side, tile_rows, tile_cols)
+    tile_real, tile_imag = forward_transform(corner, flat(grad_conv))
+    grad_taps = inverse_transform(
+        tap_table,
+        weight * jnp.sum(in_real * tile_real + in_imag * tile_imag, axis=0, keepdims=True),
+        weight * jnp.sum(in_imag * tile_real - in_real * tile_imag, axis=0, keepdims=True),
+    ).reshape(side, side, channels)
+    grad_real, grad_imag = forward_transform(whole, flat(padded_grad))
+    grad_source = inverse_transform(
+        shifted,
+        weight * (grad_real * kernel_real - grad_imag * kernel_imag),
+        weight * (grad_real * kernel_imag + grad_imag * kernel_real),
+    ).reshape(inputs.shape)
     grad_input = (
         grad_mixed + norm_backward(grad_source, gain_first, normed_first, inv_first)
     ).astype(jnp.bfloat16)

time: 1340 us -> 414 us (0.31); the launches traced: 1320 us -> 413 us
  other arithmetic: 951 us -> 21.8 us
  waiting for transfers between devices: 13.1 us -> 227 us
  local copies, waits for them, and re-layouts: 212 us -> 35 us
  loops' own time: 62.6 us -> 0 us
  matrix products: 6.6 us -> 47.4 us
    add x62 -> x0, other arithmetic: 689 us -> none  [slide_one_row(): totals + strip_rows[:, :, tap_col:tap_col + tile_cols, :] * weights_row[t...]
    reduce_sum x62 -> x0, other arithmetic: 241 us -> none  [tap_one_row(): jnp.sum(strip_rows[:, :, tap_col:tap_col + tile_cols, :].astype(jnp.float...]
    unnamed x3, waiting for transfers between devices: 0.03 us -> 184 us
    slice x124 -> x0, local copies, waits for them, and re-layouts: 137 us -> none  [slide_one_row(): weights_row[tap_col]]
    another operation x3 -> x0, loops' own time: 62.6 us -> none  [the longest x1 60.9 us: tap_sums(): return lax.map(tap_one_row, jnp.arange(side, dtype=jnp.int32))]
    dot_general x0 -> x10, matrix products: none -> 40.4 us  [the longest x4 25 us: forward_transform(): jnp.einsum('fp,bpc->bfc', table, values, preferred_element_type=jnp.float32)]
    psum x1, waiting for transfers between devices: 0.01 us -> 23.8 us  [local(): lax.psum((grad_taps, jnp.sum(grad_source * normed_first, axis=(0, 1, 2)),...]
    dynamic_update_slice x31 -> x0, local copies, waits for them, and re-layouts: 19.5 us -> none  [tap_sums(): return lax.map(tap_one_row, jnp.arange(side, dtype=jnp.int32))]
  transfers between devices with their start and end apart: 10 -> 10, of which waited for: 4 -> 8; matrix products, arithmetic and copies ran while one was open for 34% -> 14% of each run, Pallas kernels for 0% -> 0%
where the time goes in v1:
time: 414 us; the launch traced here: 413 us
  waiting for transfers between devices  227 us (55%)
  blocking collectives  48.6 us (12%)
  matrix products  47.4 us (11%)
  local copies, waits for them, and re-layouts  35 us (8%)
  other arithmetic  21.8 us (5%)
  starting transfers between devices  18.2 us (4%)
  between operations  14.7 us (4%)
    unnamed x3, waiting for transfers between devices  184 us
    psum x1, blocking collectives, local(): lax.psum((grad_taps, jnp.sum(grad_source * normed_first, axis=(0, 1, 2)),...  48.6 us
    dot_general x4, matrix products, forward_transform(): jnp.einsum('fp,bpc->bfc', table, values, preferred_element_type=jnp.float32)  25 us
    psum x1, waiting for transfers between devices, local(): lax.psum((grad_taps, jnp.sum(grad_source * normed_first, axis=(0, 1, 2)),...  23.8 us
    dot_general x6, matrix products, inverse_transform(): jnp.einsum('fp,bfc->bpc', table, spectrum, preferred_element_type=jnp.flo...  15.4 us
    unnamed x63, local copies, waits for them, and re-layouts  15 us
    ppermute x4, starting transfers between devices, padded_2(): before = lax.ppermute(last, axis, up)  12.7 us
    ppermute x4, waiting for transfers between devices, padded_2(): after = lax.ppermute(initial, axis, down)  11 us
  transfers between devices with their start and end apart: 10, of which 8 were waited for; matrix products, arithmetic and copies ran while one was open for 14% of the time, Pallas kernels for 0%

profile of v1, /device:TPU:0, one launch (start us, length us, event | category | flops | bytes accessed | tf_op | source)
XLA Modules:
  0.0 413.1 jit_solution(761380737119576861)
XLA Ops:
  10.8 4.9 %collective-permute-start = (bf16[1,15,16,512]{3,2,1,0:T(8,128)(2,1)S(1)}, bf16[1,15,16,512]{3,2,1,0:T(8,128)(2,1)S(1)}, u32[]{:S(2)}, u32[]{:S(2)}) collective-permute-start(bf16[1,15,16,512]{3,2,1,0:T(8,128)(2,1)S(1)} %get-tuple-element.46), channel_id=1, source_target_pairs={{0,16},{1,17},{2,18},{3,19},{4,20},{5,21},{6,22},{7,23},{8,24},{9,... | collective-permute-start | bytes 737288 | tf_op jit(solution)/shard_map/ppermute | solution.py:19
  17.0 3.9 collective-permute-done
  20.9 4.1 collective-permute-done.1
  33.6 6.9 %convolution_bitcast_fusion.3 = f32[1,2120,512]{2,1,0:T(8,128)} fusion(bf16[2120,961]{1,0:T(8,128)(2,1)} %constant.46.clone, bf16[961,512]{1,0:T(8,128)(2,1)} %convert_element_type.49), kind=kOutput, calls=%fused_computation.4 | convolution fusion | flops 2086215680 | bytes 9400464 | tf_op jit(solution)/shard_map/fp,bpc->bfc/dot_general | solution.py:83
  43.7 2.2 pad_maximum_fusion.1
  45.9 4.0 reshape.262
  49.9 8.8 %convolution_bitcast_fusion.1 = f32[1,2120,512]{2,1,0:T(8,128)S(1)} fusion(bf16[2116,512]{1,0:T(8,128)(2,1)} %reshape.262, bf16[2120,2116]{1,0:T(8,128)(2,1)} %constant.43.clone), kind=kOutput, calls=%fused_computation.2 | convolution fusion | flops 4593582080 | bytes 15480384 | tf_op jit(solution)/shard_map/fp,bpc->bfc/dot_general | solution.py:83
  72.1 4.5 %fusion.18 = f32[512,961]{0,1:T(8,128)S(1)} fusion(bf16[1060,961]{1,0:T(8,128)(2,1)S(1)} %copy-done.18, f32[1,2120,512]{2,1,0:T(8,128)S(1)} %convolution_bitcast_fusion.2, f32[1,2120,512]{2,1,0:T(8,128)} %copy-done.24, f32[1060]{0:T(1024)S(1)} %copy-done.23), kind=kOutput, calls=%fused_computation.35 | convolution fusion | flops 1045821440 | bytes 12871680 | tf_op jit(solution)/shard_map/fp,bfc->bpc/dot_general | solution.py:90
  80.3 2.2 fusion.56
  83.6 3.8 pad_maximum_fusion
  87.4 9.4 %copy.42 = f32[2048,1024]{1,0:T(8,128)} copy(f32[2048,1024]{0,1:T(8,128)} %pad_maximum_fusion) | data formatting | bytes 16777216
  99.5 4.3 %collective-permute-done.4 = bf16[1,15,16,512]{3,2,1,0:T(8,128)(2,1)S(1)} collective-permute-done((bf16[1,15,16,512]{3,2,1,0:T(8,128)(2,1)S(1)}, bf16[1,15,16,512]{3,2,1,0:T(8,128)(2,1)S(1)}, u32[]{:S(2)}, u32[]{:S(2)}) %collective-permute-start.4) | collective-permute-done | bytes 245792 | tf_op jit(solution)/shard_map/ppermute | solution.py:19
  103.8 3.0 collective-permute-done.5
  107.6 4.3 %collective-permute-start.6 = (bf16[1,46,15,512]{3,1,2,0:T(8,128)(2,1)S(1)}, bf16[1,46,15,512]{3,1,2,0:T(8,128)(2,1)S(1)}, u32[]{:S(2)}, u32[]{:S(2)}) collective-permute-start(bf16[1,46,15,512]{3,1,2,0:T(8,128)(2,1)S(1)} %copy.36), channel_id=1, source_target_pairs={{0,4},{4,8},{8,12},{1,5},{5,9},{9,13},{2,6},{6,10},{10,14},{3,7},{... | collective-permute-start | bytes 2119688 | tf_op jit(solution)/shard_map/ppermute | solution.py:19
  114.1 3.9 collective-permute-done.7
  118.4 2.2 pad_maximum_fusion.2
  120.6 4.0 reshape.267
  124.6 8.6 %convolution_bitcast_fusion = f32[1,2120,512]{2,1,0:T(8,128)S(1)} fusion(bf16[2116,512]{1,0:T(8,128)(2,1)} %reshape.267, bf16[2120,2116]{1,0:T(8,128)(2,1)} %constant.43.clone), kind=kOutput, calls=%fused_computation.1 | convolution fusion | flops 4593582080 | bytes 15480384 | tf_op jit(solution)/shard_map/fp,bpc->bfc/dot_general | solution.py:83
  133.3 3.4 fusion.20
  136.7 3.5 fusion.43
  140.6 48.6 %all-reduce = (f32[512]{0:T(512)S(1)}, f32[512]{0:T(512)S(1)}) all-reduce(f32[512]{0:T(512)S(1)} %get-tuple-element.32, f32[512]{0:T(512)S(1)} %get-tuple-element.30), channel_id=1, replica_groups=mesh['gy'=2,'gx'=4,'dp'=4] {'gy','gx','dp'}, use_global_device_ids=true, to_apply=%region_11.0 | all-reduce | flops 1024 | bytes 8192 | tf_op jit(solution)/shard_map/psum | solution.py:163
  192.0 23.8 %all-reduce.3.cloned.1.call-done = f32[31,31,512]{2,1,0:T(8,128)} async-done(((f32[31,31,512]{2,1,0:T(8,128)}), f32[31,31,512]{2,1,0:T(8,128)}) %all-reduce.3.cloned.1.call-update) | async-done | bytes 1968144 | tf_op jit(solution)/shard_map/psum | solution.py:163
  215.7 3.4 broadcast_multiply_fusion
  219.1 184.3 %reduce-scatter.4.cloned.1.call-done = f32[64,1024]{1,0:T(8,128)} async-done(((f32[2048,1024]{1,0:T(8,128)}), f32[64,1024]{1,0:T(8,128)}) %reduce-scatter.4.cloned.1.call-update) | async-done | bytes 262160
  (126 shorter events, 46.3 us)
Async XLA Ops:
  7.2 55.2 %copy-start = (bf16[512,2048]{1,0:T(8,128)(2,1)S(1)}, bf16[512,2048]{1,0:T(8,128)(2,1)}, u32[]{:S(2)}) copy-start(bf16[512,2048]{1,0:T(8,128)(2,1)} %param.16) | copy-start | bytes 6291460
  7.2 208.6 %all-reduce.3.cloned.1.call-start = ((), (), s32[]{:S(2)}) async-start(), calls=%async_computation.1 | async-start | bytes 4063232 | tf_op jit(solution)/shard_map/psum | solution.py:163
  10.8 10.1 %collective-permute-start = (bf16[1,15,16,512]{3,2,1,0:T(8,128)(2,1)S(1)}, bf16[1,15,16,512]{3,2,1,0:T(8,128)(2,1)S(1)}, u32[]{:S(2)}, u32[]{:S(2)}) collective-permute-start(bf16[1,15,16,512]{3,2,1,0:T(8,128)(2,1)S(1)} %get-tuple-element.46), channel_id=1, source_target_pairs={{0,16},{1,17},{2,18},{3,19},{4,20},{5,21},{6,22},{7,23},{8,24},{9,... | collective-permute-start | bytes 737288 | tf_op jit(solution)/shard_map/ppermute | solution.py:19
  15.7 9.3 %collective-permute-start.1 = (bf16[1,15,16,512]{3,2,1,0:T(8,128)(2,1)S(1)}, bf16[1,15,16,512]{3,2,1,0:T(8,128)(2,1)S(1)}, u32[]{:S(2)}, u32[]{:S(2)}) collective-permute-start(bf16[1,15,16,512]{3,2,1,0:T(8,128)(2,1)S(1)} %get-tuple-element.47), channel_id=1, source_target_pairs={{16,0},{17,1},{18,2},{19,3},{20,4},{21,5},{22,6},{23,7},{24,8},{25... | collective-permute-start | bytes 737288 | tf_op jit(solution)/shard_map/ppermute | solution.py:20
  20.9 4.1 copy-start.10
  26.2 6.0 %copy-start.8 = (f32[31,31,512]{2,1,0:T(8,128)S(1)}, f32[31,31,512]{2,1,0:T(8,128)}, u32[]{:S(2)}) copy-start(f32[31,31,512]{2,1,0:T(8,128)} %param.15) | copy-start | bytes 5904388
  27.4 13.1 %collective-permute-start.2 = (bf16[1,46,15,512]{3,1,2,0:T(8,128)(2,1)}, bf16[1,46,15,512]{3,1,2,0:T(8,128)(2,1)}, u32[]{:S(2)}, u32[]{:S(2)}) collective-permute-start(bf16[1,46,15,512]{3,1,2,0:T(8,128)(2,1)} %copy.32), channel_id=1, source_target_pairs={{0,4},{4,8},{8,12},{1,5},{5,9},{9,13},{2,6},{6,10},{10,14},{3,7},{... | collective-permute-start | bytes 2119688 | tf_op jit(solution)/shard_map/ppermute | solution.py:19
  30.9 11.2 %collective-permute-start.3 = (bf16[1,46,15,512]{3,1,2,0:T(8,128)(2,1)}, bf16[1,46,15,512]{3,1,2,0:T(8,128)(2,1)}, u32[]{:S(2)}, u32[]{:S(2)}) collective-permute-start(bf16[1,46,15,512]{3,1,2,0:T(8,128)(2,1)} %copy.33), channel_id=1, source_target_pairs={{4,0},{8,4},{12,8},{5,1},{9,5},{13,9},{6,2},{10,6},{14,10},{7,3},{... | collective-permute-start | bytes 2119688 | tf_op jit(solution)/shard_map/ppermute | solution.py:20
  45.9 12.9 %slice-start.2 = ((s8[4341760]{0:T(1024)(128)(4,1)}), s8[147456]{0:T(1024)(128)(4,1)S(1)}, s32[]{:S(2)}) async-start(s8[4341760]{0:T(1024)(128)(4,1)} %bitcast.100), calls=%async_computation.5 | async-start | bytes 294912
  49.9 8.8 %copy-start.22 = (bf16[1060,256]{1,0:T(8,128)(2,1)S(1)}, bf16[1060,256]{1,0:T(8,128)(2,1)}, u32[]{:S(2)}) copy-start(bf16[1060,256]{1,0:T(8,128)(2,1)} %constant.51) | copy-start | bytes 1628164
  49.9 8.8 %copy-start.23 = (f32[1060]{0:T(1024)S(1)}, f32[1060]{0:T(1024)}, u32[]{:S(2)}) copy-start(f32[1060]{0:T(1024)} %constant.50) | copy-start | bytes 12724
  49.9 8.8 %slice-start.3 = ((s8[4341760]{0:T(1024)(128)(4,1)}), s8[4194304]{0:T(1024)(128)(4,1)S(1)}, s32[]{:S(2)}) async-start(s8[4341760]{0:T(1024)(128)(4,1)} %bitcast.100), calls=%async_computation.6 | async-start | bytes 8388608
  70.4 6.1 %slice-start = ((s8[4341760]{0:T(1024)(128)(4,1)}), s8[4194304]{0:T(1024)(128)(4,1)S(1)}, s32[]{:S(2)}) async-start(s8[4341760]{0:T(1024)(128)(4,1)} %bitcast.98), calls=%async_computation.3 | async-start | bytes 8388608
  72.1 4.5 %copy-start.17 = (bf16[1060,961]{1,0:T(8,128)(2,1)S(1)}, bf16[1060,961]{1,0:T(8,128)(2,1)}, u32[]{:S(2)}) copy-start(bf16[1060,961]{1,0:T(8,128)(2,1)} %constant.56) | copy-start | bytes 6111964
  72.1 4.5 %slice-start.1 = ((s8[4341760]{0:T(1024)(128)(4,1)}), s8[147456]{0:T(1024)(128)(4,1)S(1)}, s32[]{:S(2)}) async-start(s8[4341760]{0:T(1024)(128)(4,1)} %bitcast.98), calls=%async_computation.4 | async-start | bytes 294912
  80.1 323.3 %reduce-scatter.4.cloned.1.call-start = ((), (), s32[]{:S(2)}) async-start(), calls=%async_computation.2 | async-start | bytes 8650752
  96.9 6.9 %collective-permute-start.4 = (bf16[1,15,16,512]{3,2,1,0:T(8,128)(2,1)S(1)}, bf16[1,15,16,512]{3,2,1,0:T(8,128)(2,1)S(1)}, u32[]{:S(2)}, u32[]{:S(2)}) collective-permute-start(bf16[1,15,16,512]{3,2,1,0:T(8,128)(2,1)S(1)} %get-tuple-element.44), channel_id=1, source_target_pairs={{0,16},{1,17},{2,18},{3,19},{4,20},{5,21},{6,22},{7,23},{8,24},{9,... | collective-permute-start | bytes 737288 | tf_op jit(solution)/shard_map/ppermute | solution.py:19
  98.2 8.6 %collective-permute-start.5 = (bf16[1,15,16,512]{3,2,1,0:T(8,128)(2,1)S(1)}, bf16[1,15,16,512]{3,2,1,0:T(8,128)(2,1)S(1)}, u32[]{:S(2)}, u32[]{:S(2)}) collective-permute-start(bf16[1,15,16,512]{3,2,1,0:T(8,128)(2,1)S(1)} %get-tuple-element.45), channel_id=1, source_target_pairs={{16,0},{17,1},{18,2},{19,3},{20,4},{21,5},{22,6},{23,7},{24,8},{25... | collective-permute-start | bytes 737288 | tf_op jit(solution)/shard_map/ppermute | solution.py:20
  107.6 6.1 %collective-permute-start.6 = (bf16[1,46,15,512]{3,1,2,0:T(8,128)(2,1)S(1)}, bf16[1,46,15,512]{3,1,2,0:T(8,128)(2,1)S(1)}, u32[]{:S(2)}, u32[]{:S(2)}) collective-permute-start(bf16[1,46,15,512]{3,1,2,0:T(8,128)(2,1)S(1)} %copy.36), channel_id=1, source_target_pairs={{0,4},{4,8},{8,12},{1,5},{5,9},{9,13},{2,6},{6,10},{10,14},{3,7},{... | collective-permute-start | bytes 2119688 | tf_op jit(solution)/shard_map/ppermute | solution.py:19
  112.4 5.6 %collective-permute-start.7 = (bf16[1,46,15,512]{3,1,2,0:T(8,128)(2,1)S(1)}, bf16[1,46,15,512]{3,1,2,0:T(8,128)(2,1)S(1)}, u32[]{:S(2)}, u32[]{:S(2)}) collective-permute-start(bf16[1,46,15,512]{3,1,2,0:T(8,128)(2,1)S(1)} %copy.37), channel_id=1, source_target_pairs={{4,0},{8,4},{12,8},{5,1},{9,5},{13,9},{6,2},{10,6},{14,10},{7,3},{... | collective-permute-start | bytes 2119688 | tf_op jit(solution)/shard_map/ppermute | solution.py:20
  124.6 8.6 %copy-start.20 = (bf16[1060,256]{1,0:T(8,128)(2,1)S(1)}, bf16[1060,256]{1,0:T(8,128)(2,1)}, u32[]{:S(2)}) copy-start(bf16[1060,256]{1,0:T(8,128)(2,1)} %constant.53) | copy-start | bytes 1628164
  133.2 3.5 copy-start.15
  133.2 3.5 copy-start.19
  215.7 190.5 %copy-start.1 = (bf16[512,2048]{1,0:T(8,128)(2,1)S(1)}, bf16[512,2048]{1,0:T(8,128)(2,1)}, u32[]{:S(2)}) copy-start(bf16[512,2048]{1,0:T(8,128)(2,1)} %param.16) | copy-start | bytes 6291460
  (15 other events, 29.9 us)
Sparse Core Ops, SparseCore 0:
  80.2 135.5 all-reduce.2
  218.1 185.2 reduce-scatter.3

commit v2 on v1

--- a/solution.py
+++ b/solution.py
@@ -92,6 +92,50 @@
 
 def flat(values):
     return values.reshape(values.shape[0], -1, values.shape[3])
+
+
+def mesh_bits(axes):
+    bits = []
+    for axis in axes:
+        bit = lax.axis_size(axis) // 2
+        while bit:
+            bits.append((axis, bit))
+            bit //= 2
+    return bits
+
+
+def swap(values, axis, bit):
+    size = lax.axis_size(axis)
+    return lax.ppermute(values, axis, [(i, i ^ bit) for i in range(size)])
+
+
+def halve(values, bits, order, wire):
+    blocks = values.reshape([2] * len(bits) + [values.shape[0] >> len(bits), values.shape[1]])
+    left = list(bits)
+    for axis, bit in order:
+        dim = left.index((axis, bit))
+        left.pop(dim)
+        mine = (lax.axis_index(axis) // bit) % 2
+        sent = lax.dynamic_index_in_dim(blocks, 1 - mine, dim, keepdims=False).astype(wire)
+        kept = lax.dynamic_index_in_dim(blocks, mine, dim, keepdims=False)
+        blocks = kept + swap(sent, axis, bit).astype(jnp.float32)
+    return blocks
+
+
+def double(block, order):
+    for axis, bit in reversed(order):
+        other = swap(block, axis, bit)
+        low = (lax.axis_index(axis) // bit) % 2 == 0
+        block = jnp.concatenate(
+            [jnp.where(low, block, other), jnp.where(low, other, block)], axis=0
+        )
+    return block
+
+
+def butterfly(values, order):
+    for axis, bit in order:
+        values = values + swap(values, axis, bit)
+    return values
 
 
 def local(features, gain_first, gain_second, kernel, up_weight, down_weight, cotangent):
@@ -131,12 +175,13 @@
     down_rows = lax.dot_general(
         activated, upstream, (((0,), (0,)), ((), ())), preferred_element_type=jnp.float32
     )
-    summed = lax.psum_scatter(
-        jnp.concatenate([up_rows, down_rows], axis=1),
-        ("gy", "gx", "dp"),
-        scatter_dimension=0,
-        tiled=True,
-    )
+    bits = mesh_bits(("gy", "gx", "dp"))
+    along = {axis: [pair for pair in bits if pair[0] == axis][::-1] for axis in ("gy", "gx", "dp")}
+    near = along["gx"][:1]
+    columns_next = near + along["gx"][1:] + along["gy"] + along["dp"]
+    rows_next = near + along["gy"] + along["gx"][1:] + along["dp"]
+    up_sum = halve(up_rows, bits, columns_next, jnp.bfloat16)
+    down_sum = halve(down_rows, bits, rows_next, jnp.bfloat16)
     grad_normed = lax.dot_general(
         grad_hidden, up_weight, (((1,), (1,)), ((), ())), preferred_element_type=jnp.float32
     ).reshape(mixed.shape)
@@ -160,22 +205,28 @@
     grad_input = (
         grad_mixed + norm_backward(grad_source, gain_first, normed_first, inv_first)
     ).astype(jnp.bfloat16)
-    small_sums = lax.psum(
-        (
-            grad_taps,
-            jnp.sum(grad_source * normed_first, axis=(0, 1, 2)),
-            jnp.sum(grad_normed * normed_second, axis=(0, 1, 2)),
-        ),
-        ("gy", "gx", "dp"),
+    gain_second_sum = jnp.sum(grad_normed * normed_second, axis=(0, 1, 2))
+    taps = side * side
+    unit = 8 << len(bits)
+    packed = jnp.concatenate(
+        [
+            grad_taps.reshape(taps, channels),
+            gain_second_sum[None],
+            jnp.zeros((-(taps + 1) % unit, channels), jnp.float32),
+        ]
+    )
+    small = double(halve(packed, columns_next, columns_next, jnp.float32), columns_next)
+    gain_first_sum = butterfly(
+        jnp.sum(grad_source * normed_first, axis=(0, 1, 2))[None], columns_next
     )
     divisor = tile_rows * lax.axis_size("gy")
     return (
         grad_input,
-        summed[:, :channels] / divisor,
-        summed[:, channels:] / divisor,
-        small_sums[0] / divisor,
-        small_sums[1] / divisor,
-        small_sums[2] / divisor,
+        up_sum / divisor,
+        down_sum / divisor,
+        small[:taps].reshape(side, side, channels) / divisor,
+        gain_first_sum[0] / divisor,
+        small[taps] / divisor,
     )
 
 

time: 414 us -> 216 us (0.52)
  waiting for transfers between devices: 227 us -> 36.3 us
  blocking collectives: 48.6 us -> 0 us
  starting transfers between devices: 18.2 us -> 59.3 us
  between operations: 14.7 us -> 1.61 us
  local copies, waits for them, and re-layouts: 35 us -> 41.7 us
    unnamed x3 -> x0, waiting for transfers between devices: 184 us -> none
    psum x1 -> x0, blocking collectives: 48.6 us -> none  [local(): lax.psum((grad_taps, jnp.sum(grad_source * normed_first, axis=(0, 1, 2)),...]
    ppermute x0 -> x25, starting transfers between devices: none -> 41.1 us  [swap(): return lax.ppermute(values, axis, [(i, i ^ bit) for i in range(size)])]
    ppermute x0 -> x25, waiting for transfers between devices: none -> 28.1 us  [swap(): return lax.ppermute(values, axis, [(i, i ^ bit) for i in range(size)])]
    psum x1 -> x0, waiting for transfers between devices: 23.8 us -> none  [local(): lax.psum((grad_taps, jnp.sum(grad_source * normed_first, axis=(0, 1, 2)),...]
    ppermute x4, waiting for transfers between devices: 11 us -> 4.39 us  [padded_2(): after = lax.ppermute(initial, axis, down)]
    add x0 -> x17, other arithmetic: none -> 6.5 us  [the longest x13 6.48 us: halve(): blocks = kept + swap(sent, axis, bit).astype(jnp.float32)]
    convert_element_type x0 -> x12, local copies, waits for them, and re-layouts: none -> 5.33 us  [the longest x10 2.56 us: halve(): lax.dynamic_index_in_dim(blocks, 1 - mine, dim, keepdims=False).astype(wire)]
  transfers between devices with their start and end apart: 10 -> 33, of which waited for: 8 -> 15; matrix products, arithmetic and copies ran while one was open for 14% -> 31% of each run, Pallas kernels for 0% -> 0%
where the time goes in v2:
time: 216 us; the launch traced here: 215 us
  starting transfers between devices  59.3 us (27%)
  matrix products  51.2 us (24%)
  local copies, waits for them, and re-layouts  41.7 us (19%)
  waiting for transfers between devices  36.3 us (17%)
  other arithmetic  24.7 us (11%)
    ppermute x25, starting transfers between devices, swap(): return lax.ppermute(values, axis, [(i, i ^ bit) for i in range(size)])  41.1 us
    ppermute x25, waiting for transfers between devices, swap(): return lax.ppermute(values, axis, [(i, i ^ bit) for i in range(size)])  28.1 us
    dot_general x4, matrix products, forward_transform(): jnp.einsum('fp,bpc->bfc', table, values, preferred_element_type=jnp.float32)  25.1 us
    dot_general x6, matrix products, inverse_transform(): jnp.einsum('fp,bfc->bpc', table, spectrum, preferred_element_type=jnp.flo...  17.7 us
    ppermute x4, starting transfers between devices, padded_2(): before = lax.ppermute(last, axis, up)  12.8 us
    unnamed x84, local copies, waits for them, and re-layouts  9.92 us
    another operation x2, local copies, waits for them, and re-layouts  8.03 us
    add x13, other arithmetic, halve(): blocks = kept + swap(sent, axis, bit).astype(jnp.float32)  6.48 us
  transfers between devices with their start and end apart: 33, of which 15 were waited for; matrix products, arithmetic and copies ran while one was open for 31% of the time, Pallas kernels for 0%

profile of v2, /device:TPU:0, one launch (start us, length us, event | category | flops | bytes accessed | tf_op | source)
XLA Modules:
  0.0 214.8 jit_solution(4372429341005714931)
XLA Ops:
  4.2 4.9 %collective-permute-start = (bf16[1,15,16,512]{3,2,1,0:T(8,128)(2,1)S(1)}, bf16[1,15,16,512]{3,2,1,0:T(8,128)(2,1)S(1)}, u32[]{:S(2)}, u32[]{:S(2)}) collective-permute-start(bf16[1,15,16,512]{3,2,1,0:T(8,128)(2,1)S(1)} %get-tuple-element.34), channel_id=1, source_target_pairs={{0,16},{1,17},{2,18},{3,19},{4,20},{5,21},{6,22},{7,23},{8,24},{9,... | collective-permute-start | bytes 737288 | tf_op jit(solution)/shard_map/ppermute | solution.py:19
  10.4 3.9 %collective-permute-done = bf16[1,15,16,512]{3,2,1,0:T(8,128)(2,1)S(1)} collective-permute-done((bf16[1,15,16,512]{3,2,1,0:T(8,128)(2,1)S(1)}, bf16[1,15,16,512]{3,2,1,0:T(8,128)(2,1)S(1)}, u32[]{:S(2)}, u32[]{:S(2)}) %collective-permute-start) | collective-permute-done | bytes 245792 | tf_op jit(solution)/shard_map/ppermute | solution.py:19
  14.3 4.1 %collective-permute-done.1 = bf16[1,15,16,512]{3,2,1,0:T(8,128)(2,1)S(1)} collective-permute-done((bf16[1,15,16,512]{3,2,1,0:T(8,128)(2,1)S(1)}, bf16[1,15,16,512]{3,2,1,0:T(8,128)(2,1)S(1)}, u32[]{:S(2)}, u32[]{:S(2)}) %collective-permute-start.1) | collective-permute-done | bytes 245792 | tf_op jit(solution)/shard_map/ppermute | solution.py:20
  30.8 7.0 %convolution_bitcast_fusion.3 = f32[1,2120,512]{2,1,0:T(8,128)} fusion(bf16[2120,961]{1,0:T(8,128)(2,1)} %constant.279.clone, bf16[961,512]{1,0:T(8,128)(2,1)} %convert_element_type.143), kind=kOutput, calls=%fused_computation.3 | convolution fusion | flops 2086215680 | bytes 9400464 | tf_op jit(solution)/shard_map/fp,bpc->bfc/dot_general | solution.py:83
  43.4 4.0 %reshape.283 = bf16[2116,512]{1,0:T(8,128)(2,1)} reshape(bf16[1,46,46,512]{3,2,1,0:T(8,128)(2,1)} %pad_maximum_fusion) | data formatting | bytes 4333568 | tf_op jit(solution)/shard_map/reshape.4
  47.4 8.6 %convolution_bitcast_fusion.1 = f32[1,2120,512]{2,1,0:T(8,128)S(1)} fusion(bf16[2116,512]{1,0:T(8,128)(2,1)} %reshape.283, bf16[2120,2116]{1,0:T(8,128)(2,1)} %constant.276.clone), kind=kOutput, calls=%fused_computation.1 | convolution fusion | flops 4593582080 | bytes 15480384 | tf_op jit(solution)/shard_map/fp,bpc->bfc/dot_general | solution.py:83
  58.2 3.3 %convolution_add_fusion.1 = f32[512,256]{0,1:T(8,128)S(1)} fusion(f32[512,256]{0,1:T(8,128)S(1)} %fusion.31, bf16[1060,256]{1,0:T(8,128)(2,1)S(1)} %copy-done.34, f32[1,2120,512]{2,1,0:T(8,128)} %convolution_bitcast_fusion.3, f32[1,2120,512]{2,1,0:T(8,128)S(1)} %convolution_bitcast_fusion.1, f32[1060]{0:T(1024)S(1)} %copy-done.36), kind=kOutput, calls=%fused_computation.41 | convolution fusion | flops 280717312 | bytes 10317824 | tf_op jit(solution)/shard_map/fp,bfc->bpc/dot_general | solution.py:90
  63.2 3.2 %multiply_convert_fusion.6 = (bf16[2048,256]{0,1:T(8,128)(2,1)}, bf16[2048,256]{0,1:T(8,128)(2,1)}, f32[256,2048]{1,0:T(8,128)S(1)}) fusion(f32[256,2048]{1,0:T(8,128)S(1)} %copy-done.17, bf16[256,512]{1,0:T(8,128)(2,1)S(1)} %bitcast.194, bf16[512,2048]{1,0:T(8,128)(2,1)S(1)} %copy-done), kind=kOutput, calls=%fused_computation.35 | convolution fusion | flops 547880960 | bytes 8650752 | tf_op jit(solution)/shard_map/dot_general | solution.py:164
  74.4 4.5 %fusion.27 = f32[512,961]{0,1:T(8,128)S(1)} fusion(bf16[1060,961]{1,0:T(8,128)(2,1)S(1)} %copy-done.31, f32[1,2120,512]{2,1,0:T(8,128)S(1)} %convolution_bitcast_fusion.2, f32[1,2120,512]{2,1,0:T(8,128)} %copy-done.37, f32[1060]{0:T(1024)S(1)} %copy-done.36), kind=kOutput, calls=%fused_computation.51 | convolution fusion | flops 1045821440 | bytes 12871680 | tf_op jit(solution)/shard_map/fp,bfc->bpc/dot_general | solution.py:90
  83.5 4.3 %collective-permute-start.6 = (bf16[1,46,15,512]{3,1,2,0:T(8,128)(2,1)}, bf16[1,46,15,512]{3,1,2,0:T(8,128)(2,1)}, u32[]{:S(2)}, u32[]{:S(2)}) collective-permute-start(bf16[1,46,15,512]{3,1,2,0:T(8,128)(2,1)} %copy.42), channel_id=1, source_target_pairs={{0,4},{4,8},{8,12},{1,5},{5,9},{9,13},{2,6},{6,10},{10,14},{3,7},{... | collective-permute-start | bytes 2119688 | tf_op jit(solution)/shard_map/ppermute | solution.py:19
  107.1 4.0 %reshape.288 = bf16[2116,512]{1,0:T(8,128)(2,1)} reshape(bf16[1,46,46,512]{3,2,1,0:T(8,128)(2,1)} %pad_maximum_fusion.1) | data formatting | bytes 4333568 | tf_op jit(solution)/shard_map/reshape.31
  111.1 8.8 %convolution_bitcast_fusion = f32[1,2120,512]{2,1,0:T(8,128)S(1)} fusion(bf16[2116,512]{1,0:T(8,128)(2,1)} %reshape.288, bf16[2120,2116]{1,0:T(8,128)(2,1)} %constant.276.clone), kind=kOutput, calls=%fused_computation | convolution fusion | flops 4593582080 | bytes 15480384 | tf_op jit(solution)/shard_map/fp,bpc->bfc/dot_general | solution.py:83
  120.0 3.4 %fusion.29 = f32[512,256]{0,1:T(8,128)S(1)} fusion(bf16[1060,256]{1,0:T(8,128)(2,1)S(1)} %copy-done.33, f32[1,2120,512]{2,1,0:T(8,128)} %convolution_bitcast_fusion.3, f32[1,2120,512]{2,1,0:T(8,128)S(1)} %convolution_bitcast_fusion, f32[1060]{0:T(1024)S(1)} %copy-done.36), kind=kOutput, calls=%fused_computation.52 | convolution fusion | flops 280586240 | bytes 9793536 | tf_op jit(solution)/shard_map/fp,bfc->bpc/dot_general | solution.py:90
  123.4 3.6 %fusion.53 = (f32[256]{0:T(256)S(1)}, f32[512,256]{0,1:T(8,128)S(1)}) fusion(f32[512]{0:T(512)S(1)} %copy-done.29, f32[512,256]{0,1:T(8,128)S(1)} %fusion.29, bf16[1060,256]{1,0:T(8,128)(2,1)S(1)} %copy-done.32, f32[1,2120,512]{2,1,0:T(8,128)} %convolution_bitcast_fusion.3, f32[1,2120,512]{2,1,0:T(8,128)S(1)} %convolution_bitcast_fusion, ...), kind=kOutput, calls=%fused_computation.90 | convolution fusion | flops 280979200 | bytes 10320896 | tf_op jit(solution)/shard_map/fp,bfc->bpc/dot_general | solution.py:90
  136.3 2.7 %collective-permute-start.30 = (f32[1,512]{1,0:T(1,128)S(1)}, f32[1,512]{1,0:T(1,128)S(1)}, u32[]{:S(2)}, u32[]{:S(2)}) collective-permute-start(f32[1,512]{1,0:T(1,128)S(1)} %add.270), channel_id=1, source_target_pairs={{0,16},{16,0},{1,17},{17,1},{2,18},{18,2},{3,19},{19,3},{4,20},{20... | collective-permute-start | bytes 6152 | tf_op jit(solution)/shard_map/ppermute | solution.py:109
  149.3 2.7 %collective-permute-start.20 = (f32[2,2,32,512]{3,2,1,0:T(8,128)S(1)}, f32[2,2,32,512]{3,2,1,0:T(8,128)S(1)}, u32[]{:S(2)}, u32[]{:S(2)}) collective-permute-start(f32[2,2,32,512]{3,2,1,0:T(8,128)S(1)} %dynamic-slice_bitcast_fusion.2), channel_id=1, source_target_pairs={{0,16},{16,0},{1,17},{17,1},{2,18},{18,2},{3,19},{19,3},{4,20},{20... | collective-permute-start | bytes 786440 | tf_op jit(solution)/shard_map/ppermute | solution.py:109
  153.7 4.1 %collective-permute-done.20 = f32[2,2,32,512]{3,2,1,0:T(8,128)S(1)} collective-permute-done((f32[2,2,32,512]{3,2,1,0:T(8,128)S(1)}, f32[2,2,32,512]{3,2,1,0:T(8,128)S(1)}, u32[]{:S(2)}, u32[]{:S(2)}) %collective-permute-start.20) | collective-permute-done | bytes 262176 | tf_op jit(solution)/shard_map/ppermute | solution.py:109
  168.3 2.8 %collective-permute-start.23 = (f32[32,512]{1,0:T(8,128)S(1)}, f32[32,512]{1,0:T(8,128)S(1)}, u32[]{:S(2)}, u32[]{:S(2)}) collective-permute-start(f32[32,512]{1,0:T(8,128)S(1)} %bitcast_add_fusion.14), channel_id=1, source_target_pairs={{0,2},{1,3},{2,0},{3,1},{4,6},{5,7},{6,4},{7,5},{8,10},{9,11},{10,... | collective-permute-start | bytes 196616 | tf_op jit(solution)/shard_map/ppermute | solution.py:109
  173.7 3.4 %collective-permute-start.24 = (f32[64,512]{1,0:T(8,128)S(1)}, f32[64,512]{1,0:T(8,128)S(1)}, u32[]{:S(2)}, u32[]{:S(2)}) collective-permute-start(f32[64,512]{1,0:T(8,128)S(1)} %pad_maximum_fusion.8), channel_id=1, source_target_pairs={{0,1},{1,0},{2,3},{3,2},{4,5},{5,4},{6,7},{7,6},{8,9},{9,8},{10,11... | collective-permute-start | bytes 393224 | tf_op jit(solution)/shard_map/ppermute | solution.py:109
  182.2 3.9 %collective-permute-done.9 = bf16[2,2,2,64,512]{4,3,2,1,0:T(8,128)(2,1)S(1)} collective-permute-done((bf16[2,2,2,64,512]{4,3,2,1,0:T(8,128)(2,1)S(1)}, bf16[2,2,2,64,512]{4,3,2,1,0:T(8,128)(2,1)S(1)}, u32[]{:S(2)}, u32[]{:S(2)}) %collective-permute-start.9) | collective-permute-done | bytes 524320 | tf_op jit(solution)/shard_map/ppermute | solution.py:109
  195.3 3.6 %collective-permute-done.26 = f32[256,512]{1,0:T(8,128)S(1)} collective-permute-done((f32[256,512]{1,0:T(8,128)S(1)}, f32[256,512]{1,0:T(8,128)S(1)}, u32[]{:S(2)}, u32[]{:S(2)}) %collective-permute-start.26) | collective-permute-done | bytes 524320 | tf_op jit(solution)/shard_map/ppermute | solution.py:109
  199.7 2.7 %collective-permute-start.12 = (bf16[64,512]{1,0:T(8,128)(2,1)S(1)}, bf16[64,512]{1,0:T(8,128)(2,1)S(1)}, u32[]{:S(2)}, u32[]{:S(2)}) collective-permute-start(bf16[64,512]{1,0:T(8,128)(2,1)S(1)} %fusion.60), channel_id=1, source_target_pairs={{0,2},{1,3},{2,0},{3,1},{4,6},{5,7},{6,4},{7,5},{8,10},{9,11},{10,... | collective-permute-start | bytes 196616 | tf_op jit(solution)/shard_map/ppermute | solution.py:109
  202.4 5.5 %collective-permute-done.17 = bf16[64,512]{1,0:T(8,128)(2,1)S(1)} collective-permute-done((bf16[64,512]{1,0:T(8,128)(2,1)S(1)}, bf16[64,512]{1,0:T(8,128)(2,1)S(1)}, u32[]{:S(2)}, u32[]{:S(2)}) %collective-permute-start.17) | collective-permute-done | bytes 65568 | tf_op jit(solution)/shard_map/ppermute | solution.py:109
  211.9 2.9 %div.105 = f32[31,31,512]{2,1,0:T(8,128)} reshape(f32[961,512]{1,0:T(8,128)} %fusion.14) | data formatting | bytes 3936256 | tf_op jit(solution)/shard_map/div | solution.py:227
  (235 shorter events, 111.3 us)
Async XLA Ops:
  4.2 10.1 %collective-permute-start = (bf16[1,15,16,512]{3,2,1,0:T(8,128)(2,1)S(1)}, bf16[1,15,16,512]{3,2,1,0:T(8,128)(2,1)S(1)}, u32[]{:S(2)}, u32[]{:S(2)}) collective-permute-start(bf16[1,15,16,512]{3,2,1,0:T(8,128)(2,1)S(1)} %get-tuple-element.34), channel_id=1, source_target_pairs={{0,16},{1,17},{2,18},{3,19},{4,20},{5,21},{6,22},{7,23},{8,24},{9,... | collective-permute-start | bytes 737288 | tf_op jit(solution)/shard_map/ppermute | solution.py:19
  9.1 9.3 %collective-permute-start.1 = (bf16[1,15,16,512]{3,2,1,0:T(8,128)(2,1)S(1)}, bf16[1,15,16,512]{3,2,1,0:T(8,128)(2,1)S(1)}, u32[]{:S(2)}, u32[]{:S(2)}) collective-permute-start(bf16[1,15,16,512]{3,2,1,0:T(8,128)(2,1)S(1)} %get-tuple-element.35), channel_id=1, source_target_pairs={{16,0},{17,1},{18,2},{19,3},{20,4},{21,5},{22,6},{23,7},{24,8},{25... | collective-permute-start | bytes 737288 | tf_op jit(solution)/shard_map/ppermute | solution.py:20
  20.9 16.9 %collective-permute-start.2 = (bf16[1,46,15,512]{3,1,2,0:T(8,128)(2,1)}, bf16[1,46,15,512]{3,1,2,0:T(8,128)(2,1)}, u32[]{:S(2)}, u32[]{:S(2)}) collective-permute-start(bf16[1,46,15,512]{3,1,2,0:T(8,128)(2,1)} %copy.38), channel_id=1, source_target_pairs={{0,4},{4,8},{8,12},{1,5},{5,9},{9,13},{2,6},{6,10},{10,14},{3,7},{... | collective-permute-start | bytes 2119688 | tf_op jit(solution)/shard_map/ppermute | solution.py:19
  24.4 15.0 %collective-permute-start.3 = (bf16[1,46,15,512]{3,1,2,0:T(8,128)(2,1)}, bf16[1,46,15,512]{3,1,2,0:T(8,128)(2,1)}, u32[]{:S(2)}, u32[]{:S(2)}) collective-permute-start(bf16[1,46,15,512]{3,1,2,0:T(8,128)(2,1)} %copy.39), channel_id=1, source_target_pairs={{4,0},{8,4},{12,8},{5,1},{9,5},{13,9},{6,2},{10,6},{14,10},{7,3},{... | collective-permute-start | bytes 2119688 | tf_op jit(solution)/shard_map/ppermute | solution.py:20
  69.7 11.1 %collective-permute-start.4 = (bf16[1,15,16,512]{3,2,1,0:T(8,128)(2,1)S(1)}, bf16[1,15,16,512]{3,2,1,0:T(8,128)(2,1)S(1)}, u32[]{:S(2)}, u32[]{:S(2)}) collective-permute-start(bf16[1,15,16,512]{3,2,1,0:T(8,128)(2,1)S(1)} %get-tuple-element.32), channel_id=1, source_target_pairs={{0,16},{1,17},{2,18},{3,19},{4,20},{5,21},{6,22},{7,23},{8,24},{9,... | collective-permute-start | bytes 737288 | tf_op jit(solution)/shard_map/ppermute | solution.py:19
  71.2 9.9 %collective-permute-start.5 = (bf16[1,15,16,512]{3,2,1,0:T(8,128)(2,1)S(1)}, bf16[1,15,16,512]{3,2,1,0:T(8,128)(2,1)S(1)}, u32[]{:S(2)}, u32[]{:S(2)}) collective-permute-start(bf16[1,15,16,512]{3,2,1,0:T(8,128)(2,1)S(1)} %get-tuple-element.33), channel_id=1, source_target_pairs={{16,0},{17,1},{18,2},{19,3},{20,4},{21,5},{22,6},{23,7},{24,8},{25... | collective-permute-start | bytes 737288 | tf_op jit(solution)/shard_map/ppermute | solution.py:20
  83.5 18.4 %collective-permute-start.6 = (bf16[1,46,15,512]{3,1,2,0:T(8,128)(2,1)}, bf16[1,46,15,512]{3,1,2,0:T(8,128)(2,1)}, u32[]{:S(2)}, u32[]{:S(2)}) collective-permute-start(bf16[1,46,15,512]{3,1,2,0:T(8,128)(2,1)} %copy.42), channel_id=1, source_target_pairs={{0,4},{4,8},{8,12},{1,5},{5,9},{9,13},{2,6},{6,10},{10,14},{3,7},{... | collective-permute-start | bytes 2119688 | tf_op jit(solution)/shard_map/ppermute | solution.py:19
  89.1 14.3 %collective-permute-start.7 = (bf16[1,46,15,512]{3,1,2,0:T(8,128)(2,1)}, bf16[1,46,15,512]{3,1,2,0:T(8,128)(2,1)}, u32[]{:S(2)}, u32[]{:S(2)}) collective-permute-start(bf16[1,46,15,512]{3,1,2,0:T(8,128)(2,1)} %copy.43), channel_id=1, source_target_pairs={{4,0},{8,4},{12,8},{5,1},{9,5},{13,9},{6,2},{10,6},{14,10},{7,3},{... | collective-permute-start | bytes 2119688 | tf_op jit(solution)/shard_map/ppermute | solution.py:20
  93.1 37.2 %collective-permute-start.18 = (f32[2,2,2,2,32,512]{5,4,3,2,1,0:T(8,128)}, f32[2,2,2,2,32,512]{5,4,3,2,1,0:T(8,128)}, u32[]{:S(2)}, u32[]{:S(2)}) collective-permute-start(f32[2,2,2,2,32,512]{5,4,3,2,1,0:T(8,128)} %dynamic-slice_bitcast_fusion), channel_id=1, source_target_pairs={{0,4},{4,0},{8,12},{12,8},{1,5},{5,1},{9,13},{13,9},{2,6},{6,2},{1... | collective-permute-start | bytes 3145736 | tf_op jit(solution)/shard_map/ppermute | solution.py:109
  100.1 59.4 %collective-permute-start.13 = (bf16[2,2,2,2,64,512]{5,4,2,3,1,0:T(8,128)(2,1)}, bf16[2,2,2,2,64,512]{5,4,2,3,1,0:T(8,128)(2,1)}, u32[]{:S(2)}, u32[]{:S(2)}) collective-permute-start(bf16[2,2,2,2,64,512]{5,4,2,3,1,0:T(8,128)(2,1)} %fusion.34), channel_id=1, source_target_pairs={{0,4},{4,0},{8,12},{12,8},{1,5},{5,1},{9,13},{13,9},{2,6},{6,2},{1... | collective-permute-start | bytes 3145736 | tf_op jit(solution)/shard_map/ppermute | solution.py:109
  128.6 7.7 %collective-permute-start.29 = (f32[1,512]{1,0:T(1,128)S(1)}, f32[1,512]{1,0:T(1,128)S(1)}, u32[]{:S(2)}, u32[]{:S(2)}) collective-permute-start(f32[1,512]{1,0:T(1,128)S(1)} %add.269), channel_id=1, source_target_pairs={{0,8},{4,12},{8,0},{12,4},{1,9},{5,13},{9,1},{13,5},{2,10},{6,14},... | collective-permute-start | bytes 6152 | tf_op jit(solution)/shard_map/ppermute | solution.py:109
  133.7 14.3 %collective-permute-start.19 = (f32[2,2,2,32,512]{4,3,2,1,0:T(8,128)}, f32[2,2,2,32,512]{4,3,2,1,0:T(8,128)}, u32[]{:S(2)}, u32[]{:S(2)}) collective-permute-start(f32[2,2,2,32,512]{4,3,2,1,0:T(8,128)} %dynamic-slice_bitcast_fusion.1), channel_id=1, source_target_pairs={{0,8},{4,12},{8,0},{12,4},{1,9},{5,13},{9,1},{13,5},{2,10},{6,14},... | collective-permute-start | bytes 1572872 | tf_op jit(solution)/shard_map/ppermute | solution.py:109
  136.2 29.6 %collective-permute-start.8 = (bf16[2,2,2,2,64,512]{5,4,3,2,1,0:T(8,128)(2,1)}, bf16[2,2,2,2,64,512]{5,4,3,2,1,0:T(8,128)(2,1)}, u32[]{:S(2)}, u32[]{:S(2)}) collective-permute-start(bf16[2,2,2,2,64,512]{5,4,3,2,1,0:T(8,128)(2,1)} %fusion.33), channel_id=1, source_target_pairs={{0,4},{4,0},{8,12},{12,8},{1,5},{5,1},{9,13},{13,9},{2,6},{6,2},{1... | collective-permute-start | bytes 3145736 | tf_op jit(solution)/shard_map/ppermute | solution.py:109
  144.2 8.9 %collective-permute-start.32 = (f32[1,512]{1,0:T(1,128)S(1)}, f32[1,512]{1,0:T(1,128)S(1)}, u32[]{:S(2)}, u32[]{:S(2)}) collective-permute-start(f32[1,512]{1,0:T(1,128)S(1)} %add.272), channel_id=1, source_target_pairs={{0,2},{1,3},{2,0},{3,1},{4,6},{5,7},{6,4},{7,5},{8,10},{9,11},{10,... | collective-permute-start | bytes 6152 | tf_op jit(solution)/shard_map/ppermute | solution.py:109
  149.3 8.5 %collective-permute-start.20 = (f32[2,2,32,512]{3,2,1,0:T(8,128)S(1)}, f32[2,2,32,512]{3,2,1,0:T(8,128)S(1)}, u32[]{:S(2)}, u32[]{:S(2)}) collective-permute-start(f32[2,2,32,512]{3,2,1,0:T(8,128)S(1)} %dynamic-slice_bitcast_fusion.2), channel_id=1, source_target_pairs={{0,16},{16,0},{1,17},{17,1},{2,18},{18,2},{3,19},{19,3},{4,20},{20... | collective-permute-start | bytes 786440 | tf_op jit(solution)/shard_map/ppermute | solution.py:109
  161.2 15.8 %collective-permute-start.14 = (bf16[2,2,2,64,512]{4,3,1,2,0:T(8,128)(2,1)S(1)}, bf16[2,2,2,64,512]{4,3,1,2,0:T(8,128)(2,1)S(1)}, u32[]{:S(2)}, u32[]{:S(2)}) collective-permute-start(bf16[2,2,2,64,512]{4,3,1,2,0:T(8,128)(2,1)S(1)} %fusion.52), channel_id=1, source_target_pairs={{0,16},{16,0},{1,17},{17,1},{2,18},{18,2},{3,19},{19,3},{4,20},{20... | collective-permute-start | bytes 1572872 | tf_op jit(solution)/shard_map/ppermute | solution.py:109
  171.2 14.9 %collective-permute-start.9 = (bf16[2,2,2,64,512]{4,3,2,1,0:T(8,128)(2,1)S(1)}, bf16[2,2,2,64,512]{4,3,2,1,0:T(8,128)(2,1)S(1)}, u32[]{:S(2)}, u32[]{:S(2)}) collective-permute-start(bf16[2,2,2,64,512]{4,3,2,1,0:T(8,128)(2,1)S(1)} %fusion.51), channel_id=1, source_target_pairs={{0,8},{4,12},{8,0},{12,4},{1,9},{5,13},{9,1},{13,5},{2,10},{6,14},... | collective-permute-start | bytes 1572872 | tf_op jit(solution)/shard_map/ppermute | solution.py:109
  177.3 14.4 %collective-permute-start.15 = (bf16[2,2,64,512]{3,2,0,1:T(8,128)(2,1)S(1)}, bf16[2,2,64,512]{3,2,0,1:T(8,128)(2,1)S(1)}, u32[]{:S(2)}, u32[]{:S(2)}) collective-permute-start(bf16[2,2,64,512]{3,2,0,1:T(8,128)(2,1)S(1)} %fusion.55), channel_id=1, source_target_pairs={{0,8},{4,12},{8,0},{12,4},{1,9},{5,13},{9,1},{13,5},{2,10},{6,14},... | collective-permute-start | bytes 786440 | tf_op jit(solution)/shard_map/ppermute | solution.py:109
  186.3 7.9 %collective-permute-start.10 = (bf16[2,2,64,512]{3,2,1,0:T(8,128)(2,1)S(1)}, bf16[2,2,64,512]{3,2,1,0:T(8,128)(2,1)S(1)}, u32[]{:S(2)}, u32[]{:S(2)}) collective-permute-start(bf16[2,2,64,512]{3,2,1,0:T(8,128)(2,1)S(1)} %fusion.54), channel_id=1, source_target_pairs={{0,16},{16,0},{1,17},{17,1},{2,18},{18,2},{3,19},{19,3},{4,20},{20... | collective-permute-start | bytes 786440 | tf_op jit(solution)/shard_map/ppermute | solution.py:109
  187.2 11.7 %collective-permute-start.26 = (f32[256,512]{1,0:T(8,128)S(1)}, f32[256,512]{1,0:T(8,128)S(1)}, u32[]{:S(2)}, u32[]{:S(2)}) collective-permute-start(f32[256,512]{1,0:T(8,128)S(1)} %pad_maximum_fusion.6), channel_id=1, source_target_pairs={{0,8},{4,12},{8,0},{12,4},{1,9},{5,13},{9,1},{13,5},{2,10},{6,14},... | collective-permute-start | bytes 1572872 | tf_op jit(solution)/shard_map/ppermute | solution.py:109
  191.8 7.4 %collective-permute-start.16 = (bf16[2,64,512]{2,1,0:T(8,128)(2,1)S(1)}, bf16[2,64,512]{2,1,0:T(8,128)(2,1)S(1)}, u32[]{:S(2)}, u32[]{:S(2)}) collective-permute-start(bf16[2,64,512]{2,1,0:T(8,128)(2,1)S(1)} %fusion.57), channel_id=1, source_target_pairs={{0,1},{1,0},{2,3},{3,2},{4,5},{5,4},{6,7},{7,6},{8,9},{9,8},{10,11... | collective-permute-start | bytes 393224 | tf_op jit(solution)/shard_map/ppermute | solution.py:109
  199.1 10.5 %collective-permute-start.27 = (f32[512,512]{1,0:T(8,128)S(1)}, f32[512,512]{1,0:T(8,128)S(1)}, u32[]{:S(2)}, u32[]{:S(2)}) collective-permute-start(f32[512,512]{1,0:T(8,128)S(1)} %pad_maximum_fusion.3), channel_id=1, source_target_pairs={{0,4},{4,0},{8,12},{12,8},{1,5},{5,1},{9,13},{13,9},{2,6},{6,2},{1... | collective-permute-start | bytes 3145736 | tf_op jit(solution)/shard_map/ppermute | solution.py:109
  199.3 8.7 %collective-permute-start.17 = (bf16[64,512]{1,0:T(8,128)(2,1)S(1)}, bf16[64,512]{1,0:T(8,128)(2,1)S(1)}, u32[]{:S(2)}, u32[]{:S(2)}) collective-permute-start(bf16[64,512]{1,0:T(8,128)(2,1)S(1)} %fusion.61), channel_id=1, source_target_pairs={{0,2},{1,3},{2,0},{3,1},{4,6},{5,7},{6,4},{7,5},{8,10},{9,11},{10,... | collective-permute-start | bytes 196616 | tf_op jit(solution)/shard_map/ppermute | solution.py:109
  199.7 9.2 %collective-permute-start.12 = (bf16[64,512]{1,0:T(8,128)(2,1)S(1)}, bf16[64,512]{1,0:T(8,128)(2,1)S(1)}, u32[]{:S(2)}, u32[]{:S(2)}) collective-permute-start(bf16[64,512]{1,0:T(8,128)(2,1)S(1)} %fusion.60), channel_id=1, source_target_pairs={{0,2},{1,3},{2,0},{3,1},{4,6},{5,7},{6,4},{7,5},{8,10},{9,11},{10,... | collective-permute-start | bytes 196616 | tf_op jit(solution)/shard_map/ppermute | solution.py:109
  (51 other events, 314.1 us)

commit v3 on v2

--- a/solution.py
+++ b/solution.py
@@ -49,8 +49,13 @@
     )
 
 
-def extend(source, reach):
-    return padded_2(source, (("gy", 1), ("gx", 2)), reach)
+def extend_rows(source, reach):
+    return padded_2(source, (("gy", 1),), reach)
+
+
+def extend_cols(source, reach):
+    wide = padded_2(source, (("gx", 2),), reach)
+    return jnp.pad(wide, ((0, 0), (0, 0), (0, -wide.shape[2] % 16), (0, 0)))
 
 
 def transform_tables(tile_rows, tile_cols, side):
@@ -72,7 +77,7 @@
         angle = angle.reshape(len(freqs), -1)
         return jnp.asarray(np.concatenate([np.cos(angle), -np.sin(angle)]), jnp.bfloat16)
 
-    whole = table(np.arange(rows), np.arange(cols))
+    whole = table(np.arange(rows), np.arange(cols + -cols % 16))
     corner = table(np.arange(tile_rows), np.arange(tile_cols))
     shifted = table(np.arange(tile_rows) + side - 1, np.arange(tile_cols) + side - 1)
     taps = table(np.arange(side), np.arange(side))
@@ -109,33 +114,23 @@
     return lax.ppermute(values, axis, [(i, i ^ bit) for i in range(size)])
 
 
-def halve(values, bits, order, wire):
-    blocks = values.reshape([2] * len(bits) + [values.shape[0] >> len(bits), values.shape[1]])
-    left = list(bits)
-    for axis, bit in order:
-        dim = left.index((axis, bit))
-        left.pop(dim)
-        mine = (lax.axis_index(axis) // bit) % 2
-        sent = lax.dynamic_index_in_dim(blocks, 1 - mine, dim, keepdims=False).astype(wire)
-        kept = lax.dynamic_index_in_dim(blocks, mine, dim, keepdims=False)
-        blocks = kept + swap(sent, axis, bit).astype(jnp.float32)
-    return blocks
-
-
-def double(block, order):
-    for axis, bit in reversed(order):
-        other = swap(block, axis, bit)
-        low = (lax.axis_index(axis) // bit) % 2 == 0
-        block = jnp.concatenate(
-            [jnp.where(low, block, other), jnp.where(low, other, block)], axis=0
-        )
-    return block
-
-
-def butterfly(values, order):
-    for axis, bit in order:
-        values = values + swap(values, axis, bit)
-    return values
+def blocked(values, bits):
+    return values.reshape([2] * len(bits) + [values.shape[0] >> len(bits), values.shape[1]])
+
+
+def halve(blocks, bits, order, step, wire):
+    axis, bit = order[step]
+    dim = [pair for pair in bits if pair not in order[:step]].index((axis, bit))
+    mine = (lax.axis_index(axis) // bit) % 2
+    sent = lax.dynamic_index_in_dim(blocks, 1 - mine, dim, keepdims=False).astype(wire)
+    kept = lax.dynamic_index_in_dim(blocks, mine, dim, keepdims=False)
+    return kept + swap(sent, axis, bit).astype(jnp.float32)
+
+
+def double(block, axis, bit):
+    other = swap(block, axis, bit)
+    low = (lax.axis_index(axis) // bit) % 2 == 0
+    return jnp.concatenate([jnp.where(low, block, other), jnp.where(low, other, block)], axis=0)
 
 
 def local(features, gain_first, gain_second, kernel, up_weight, down_weight, cotangent):
@@ -147,7 +142,7 @@
     inputs = features.astype(jnp.float32)
     first, normed_first, inv_first = norm_forward(inputs, gain_first)
     conv_in = first.astype(jnp.bfloat16)
-    padded_in = extend(conv_in, reach)
+    padded_in = extend_cols(extend_rows(conv_in, reach), reach)
     whole, corner, shifted, tap_table, weight = transform_tables(tile_rows, tile_cols, side)
     kernel_real, kernel_imag = forward_transform(
         tap_table, kernel.reshape(1, side * side, channels).astype(jnp.bfloat16)
@@ -180,8 +175,16 @@
     near = along["gx"][:1]
     columns_next = near + along["gx"][1:] + along["gy"] + along["dp"]
     rows_next = near + along["gy"] + along["gx"][1:] + along["dp"]
-    up_sum = halve(up_rows, bits, columns_next, jnp.bfloat16)
-    down_sum = halve(down_rows, bits, rows_next, jnp.bfloat16)
+    steps = len(bits)
+    up_sum = blocked(up_rows, bits)
+    down_sum = blocked(down_rows, bits)
+
+    def up_step(blocks, step):
+        return halve(blocks, bits, columns_next, step, jnp.bfloat16) if step < steps else blocks
+
+    def down_step(blocks, step):
+        return halve(blocks, bits, rows_next, step, jnp.bfloat16) if step < steps else blocks
+
     grad_normed = lax.dot_general(
         grad_hidden, up_weight, (((1,), (1,)), ((), ())), preferred_element_type=jnp.float32
     ).reshape(mixed.shape)
@@ -189,36 +192,68 @@
         grad_normed, gain_second, normed_second, inv_second
     )
     grad_conv = grad_mixed.astype(jnp.bfloat16)
-    padded_grad = extend(grad_conv, reach)
+    fence = lax.optimization_barrier
+    taps = side * side
+    up_sum = up_step(up_sum, 0)
+    down_sum = down_step(down_sum, 0)
+    tall_grad = extend_rows(grad_conv, reach)
     tile_real, tile_imag = forward_transform(corner, flat(grad_conv))
     grad_taps = inverse_transform(
         tap_table,
         weight * jnp.sum(in_real * tile_real + in_imag * tile_imag, axis=0, keepdims=True),
         weight * jnp.sum(in_imag * tile_real - in_real * tile_imag, axis=0, keepdims=True),
-    ).reshape(side, side, channels)
+    )
+    gain_second_sum = jnp.sum(grad_normed * normed_second, axis=(0, 1, 2))
+    small = jnp.concatenate(
+        [
+            grad_taps[0],
+            gain_second_sum[None],
+            jnp.zeros((-(taps + 1) % (8 << steps), channels), jnp.float32),
+        ]
+    )
+    small = blocked(small, bits)
+    tall_grad, small, up_sum, down_sum = fence((tall_grad, small, up_sum, down_sum))
+
+    small = halve(small, columns_next, columns_next, 0, jnp.float32)
+    padded_grad = extend_cols(tall_grad, reach)
+    up_sum = up_step(up_sum, 1)
+    down_sum = down_step(down_sum, 1)
+    padded_grad, small, up_sum, down_sum = fence((padded_grad, small, up_sum, down_sum))
+
+    small = halve(small, columns_next, columns_next, 1, jnp.float32)
+    up_sum = up_step(up_sum, 2)
+    down_sum = down_step(down_sum, 2)
     grad_real, grad_imag = forward_transform(whole, flat(padded_grad))
-    grad_source = inverse_transform(
-        shifted,
-        weight * (grad_real * kernel_real - grad_imag * kernel_imag),
-        weight * (grad_real * kernel_imag + grad_imag * kernel_real),
-    ).reshape(inputs.shape)
+    product_real = weight * (grad_real * kernel_real - grad_imag * kernel_imag)
+    product_imag = weight * (grad_real * kernel_imag + grad_imag * kernel_real)
+    product_real, product_imag, small, up_sum, down_sum = fence(
+        (
+            product_real.astype(jnp.bfloat16),
+            product_imag.astype(jnp.bfloat16),
+            small,
+            up_sum,
+            down_sum,
+        )
+    )
+
+    small = halve(small, columns_next, columns_next, 2, jnp.float32)
+    up_sum = up_step(up_sum, 3)
+    down_sum = down_step(down_sum, 3)
+    grad_source = inverse_transform(shifted, product_real, product_imag).reshape(inputs.shape)
     grad_input = (
         grad_mixed + norm_backward(grad_source, gain_first, normed_first, inv_first)
     ).astype(jnp.bfloat16)
-    gain_second_sum = jnp.sum(grad_normed * normed_second, axis=(0, 1, 2))
-    taps = side * side
-    unit = 8 << len(bits)
-    packed = jnp.concatenate(
-        [
-            grad_taps.reshape(taps, channels),
-            gain_second_sum[None],
-            jnp.zeros((-(taps + 1) % unit, channels), jnp.float32),
-        ]
-    )
-    small = double(halve(packed, columns_next, columns_next, jnp.float32), columns_next)
-    gain_first_sum = butterfly(
-        jnp.sum(grad_source * normed_first, axis=(0, 1, 2))[None], columns_next
-    )
+    gain_first_sum = jnp.sum(grad_source * normed_first, axis=(0, 1, 2))[None]
+    gain_first_sum, small, up_sum, down_sum = fence((gain_first_sum, small, up_sum, down_sum))
+
+    for step in range(4, steps):
+        up_sum = up_step(up_sum, step)
+        down_sum = down_step(down_sum, step)
+    for step in range(3, steps):
+        small = halve(small, columns_next, columns_next, step, jnp.float32)
+    for axis, bit in reversed(columns_next):
+        small = double(small, axis, bit)
+        gain_first_sum = gain_first_sum + swap(gain_first_sum, axis, bit)
     divisor = tile_rows * lax.axis_size("gy")
     return (
         grad_input,

time: 216 us -> 215 us (level)
  waiting for transfers between devices: 36.3 us -> 55.6 us
  matrix products: 51.2 us -> 39.6 us
  local copies, waits for them, and re-layouts: 41.7 us -> 33.1 us
  other arithmetic: 24.7 us -> 28 us
  starting transfers between devices: 59.3 us -> 56.5 us
    ppermute x25, waiting for transfers between devices: 28.1 us -> 50.4 us  [swap(): return lax.ppermute(values, axis, [(i, i ^ bit) for i in range(size)])]
    dot_general x6 -> x5, matrix products: 17.7 us -> 9.37 us  [inverse_transform(): jnp.einsum('fp,bfc->bpc', table, spectrum, preferred_element_type=jnp.flo...]
    another operation x2 -> x0, local copies, waits for them, and re-layouts: 8.03 us -> none
    ppermute x25, starting transfers between devices: 41.1 us -> 33.4 us  [swap(): return lax.ppermute(values, axis, [(i, i ^ bit) for i in range(size)])]
    ppermute x4, starting transfers between devices: 12.8 us -> 18 us  [padded_2(): before = lax.ppermute(last, axis, up)]
    dot_general x4, matrix products: 25.1 us -> 21.9 us  [forward_transform(): jnp.einsum('fp,bpc->bfc', table, values, preferred_element_type=jnp.float32)]
    ppermute x4, waiting for transfers between devices: 3.89 us -> 1.2 us  [padded_2(): before = lax.ppermute(last, axis, up)]
    unnamed x84 -> x80, local copies, waits for them, and re-layouts: 9.92 us -> 8.38 us
  transfers between devices with their start and end apart: 33 -> 33, of which waited for: 15 -> 18; matrix products, arithmetic and copies ran while one was open for 31% -> 23% of each run, Pallas kernels for 0% -> 0%
where the time goes in v3:
time: 215 us; the launch traced here: 214 us
  starting transfers between devices  56.5 us (26%)
  waiting for transfers between devices  55.6 us (26%)
  matrix products  39.6 us (18%)
  local copies, waits for them, and re-layouts  33.1 us (15%)
  other arithmetic  28 us (13%)
    ppermute x25, waiting for transfers between devices, swap(): return lax.ppermute(values, axis, [(i, i ^ bit) for i in range(size)])  50.4 us
    ppermute x25, starting transfers between devices, swap(): return lax.ppermute(values, axis, [(i, i ^ bit) for i in range(size)])  33.4 us
    dot_general x4, matrix products, forward_transform(): jnp.einsum('fp,bpc->bfc', table, values, preferred_element_type=jnp.float32)  21.9 us
    ppermute x4, starting transfers between devices, padded_2(): before = lax.ppermute(last, axis, up)  18 us
    dot_general x5, matrix products, inverse_transform(): jnp.einsum('fp,bfc->bpc', table, spectrum, preferred_element_type=jnp.flo...  9.37 us
    unnamed x80, local copies, waits for them, and re-layouts  8.38 us
    add x13, other arithmetic, halve(): return kept + swap(sent, axis, bit).astype(jnp.float32)  7.91 us
    ppermute x4, starting transfers between devices, padded_2(): after = lax.ppermute(initial, axis, down)  5.13 us
  transfers between devices with their start and end apart: 33, of which 18 were waited for; matrix products, arithmetic and copies ran while one was open for 23% of the time, Pallas kernels for 0%

profile of v3, /device:TPU:0, one launch (start us, length us, event | category | flops | bytes accessed | tf_op | source)
XLA Modules:
  0.0 214.4 jit_solution(15590943532308740432)
XLA Ops:
  5.5 4.9 %collective-permute-start = (bf16[1,15,16,512]{3,2,1,0:T(8,128)(2,1)S(1)}, bf16[1,15,16,512]{3,2,1,0:T(8,128)(2,1)S(1)}, u32[]{:S(2)}, u32[]{:S(2)}) collective-permute-start(bf16[1,15,16,512]{3,2,1,0:T(8,128)(2,1)S(1)} %get-tuple-element.70), channel_id=1, source_target_pairs={{0,16},{1,17},{2,18},{3,19},{4,20},{5,21},{6,22},{7,23},{8,24},{9,... | collective-permute-start | bytes 737288 | tf_op jit(solution)/shard_map/ppermute | solution.py:19
  10.4 4.0 %collective-permute-done.1 = bf16[1,15,16,512]{3,2,1,0:T(8,128)(2,1)S(1)} collective-permute-done((bf16[1,15,16,512]{3,2,1,0:T(8,128)(2,1)S(1)}, bf16[1,15,16,512]{3,2,1,0:T(8,128)(2,1)S(1)}, u32[]{:S(2)}, u32[]{:S(2)}) %collective-permute-start.1) | collective-permute-done | bytes 245792 | tf_op jit(solution)/shard_map/ppermute | solution.py:20
  20.7 3.9 %collective-permute-start.2 = (bf16[1,46,15,512]{3,1,2,0:T(8,128)(2,1)}, bf16[1,46,15,512]{3,1,2,0:T(8,128)(2,1)}, u32[]{:S(2)}, u32[]{:S(2)}) collective-permute-start(bf16[1,46,15,512]{3,1,2,0:T(8,128)(2,1)} %copy.38), channel_id=1, source_target_pairs={{0,4},{4,8},{8,12},{1,5},{5,9},{9,13},{2,6},{6,10},{10,14},{3,7},{... | collective-permute-start | bytes 2119688 | tf_op jit(solution)/shard_map/ppermute | solution.py:19
  29.8 5.0 %convolution_bitcast_fusion.3 = f32[1,2120,512]{2,1,0:T(8,128)S(1)} fusion(bf16[2120,961]{1,0:T(8,128)(2,1)} %constant.281.clone, bf16[961,512]{1,0:T(8,128)(2,1)} %convert_element_type.148), kind=kOutput, calls=%fused_computation.3 | convolution fusion | flops 2086215680 | bytes 9400464 | tf_op jit(solution)/shard_map/fp,bpc->bfc/dot_general | solution.py:88
  40.0 7.9 %convolution_bitcast_fusion.1 = f32[1,2120,512]{2,1,0:T(8,128)S(1)} fusion(bf16[2208,512]{1,0:T(8,128)(2,1)S(1)} %bitcast.195, bf16[2120,2208]{1,0:T(8,128)(2,1)} %constant.278.clone), kind=kOutput, calls=%fused_computation.1 | convolution fusion | flops 4793303040 | bytes 15964672 | tf_op jit(solution)/shard_map/fp,bpc->bfc/dot_general | solution.py:88
  52.7 3.2 %multiply_convert_fusion.6 = (bf16[2048,256]{0,1:T(8,128)(2,1)}, bf16[2048,256]{0,1:T(8,128)(2,1)}, f32[256,2048]{1,0:T(8,128)S(1)}) fusion(f32[256,2048]{1,0:T(8,128)S(1)} %copy-done.16, bf16[256,512]{1,0:T(8,128)(2,1)S(1)} %bitcast.196, bf16[512,2048]{1,0:T(8,128)(2,1)S(1)} %copy-done), kind=kOutput, calls=%fused_computation.52 | convolution fusion | flops 547880960 | bytes 8650752 | tf_op jit(solution)/shard_map/dot_general | solution.py:159
  61.3 5.3 %collective-permute-start.4 = (bf16[1,15,16,512]{3,2,1,0:T(8,128)(2,1)S(1)}, bf16[1,15,16,512]{3,2,1,0:T(8,128)(2,1)}, u32[]{:S(2)}, u32[]{:S(2)}) collective-permute-start(bf16[1,15,16,512]{3,2,1,0:T(8,128)(2,1)S(1)} %get-tuple-element.68), channel_id=1, source_target_pairs={{0,16},{1,17},{2,18},{3,19},{4,20},{5,21},{6,22},{7,23},{8,24},{9,... | collective-permute-start | bytes 737288 | tf_op jit(solution)/shard_map/ppermute | solution.py:19
  77.7 4.5 %fusion.40 = f32[512,961]{0,1:T(8,128)S(1)} fusion(bf16[1060,961]{1,0:T(8,128)(2,1)S(1)} %copy-done.31, f32[1,2120,512]{2,1,0:T(8,128)S(1)} %convolution_bitcast_fusion.2, f32[1,2120,512]{2,1,0:T(8,128)} %copy-done.35, f32[1060]{0:T(1024)S(1)} %copy-done.29), kind=kOutput, calls=%fused_computation.64 | convolution fusion | flops 1045821440 | bytes 12871680 | tf_op jit(solution)/shard_map/fp,bfc->bpc/dot_general | solution.py:95
  98.3 3.9 %collective-permute-start.8 = (bf16[1,46,15,512]{3,1,2,0:T(8,128)(2,1)}, bf16[1,46,15,512]{3,1,2,0:T(8,128)(2,1)}, u32[]{:S(2)}, u32[]{:S(2)}) collective-permute-start(bf16[1,46,15,512]{3,1,2,0:T(8,128)(2,1)} %copy.46), channel_id=1, source_target_pairs={{0,4},{4,8},{8,12},{1,5},{5,9},{9,13},{2,6},{6,10},{10,14},{3,7},{... | collective-permute-start | bytes 2119688 | tf_op jit(solution)/shard_map/ppermute | solution.py:19
  102.3 3.3 %collective-permute-done.11 = bf16[2,2,2,64,512]{4,3,2,1,0:T(8,128)(2,1)} collective-permute-done((bf16[2,2,2,64,512]{4,3,2,1,0:T(8,128)(2,1)S(1)}, bf16[2,2,2,64,512]{4,3,2,1,0:T(8,128)(2,1)}, u32[]{:S(2)}, u32[]{:S(2)}) %collective-permute-start.11) | collective-permute-done | bytes 524320 | tf_op jit(solution)/shard_map/ppermute | solution.py:114
  115.3 8.3 %convolution_bitcast_fusion = f32[1,2120,512]{2,1,0:T(8,128)S(1)} fusion(bf16[2208,512]{1,0:T(8,128)(2,1)S(1)} %bitcast.194, bf16[2120,2208]{1,0:T(8,128)(2,1)} %constant.278.clone), kind=kOutput, calls=%fused_computation | convolution fusion | flops 4793303040 | bytes 15964672 | tf_op jit(solution)/shard_map/fp,bpc->bfc/dot_general | solution.py:88
  123.6 4.4 %collective-permute-start.13 = (f32[2,2,2,32,512]{4,3,2,1,0:T(8,128)S(1)}, f32[2,2,2,32,512]{4,3,2,1,0:T(8,128)S(1)}, u32[]{:S(2)}, u32[]{:S(2)}) collective-permute-start(f32[2,2,2,32,512]{4,3,2,1,0:T(8,128)S(1)} %dynamic-slice_bitcast_fusion.1), channel_id=1, source_target_pairs={{0,8},{4,12},{8,0},{12,4},{1,9},{5,13},{9,1},{13,5},{2,10},{6,14},... | collective-permute-start | bytes 1572872 | tf_op jit(solution)/shard_map/ppermute | solution.py:114
  129.3 6.7 %collective-permute-done.14 = bf16[2,2,64,512]{3,2,1,0:T(8,128)(2,1)S(1)} collective-permute-done((bf16[2,2,64,512]{3,2,1,0:T(8,128)(2,1)S(1)}, bf16[2,2,64,512]{3,2,1,0:T(8,128)(2,1)S(1)}, u32[]{:S(2)}, u32[]{:S(2)}) %collective-permute-start.14) | collective-permute-done | bytes 262176 | tf_op jit(solution)/shard_map/ppermute | solution.py:114
  136.1 9.7 %collective-permute-done.15 = bf16[2,2,64,512]{3,2,0,1:T(8,128)(2,1)S(1)} collective-permute-done((bf16[2,2,64,512]{3,2,0,1:T(8,128)(2,1)S(1)}, bf16[2,2,64,512]{3,2,0,1:T(8,128)(2,1)S(1)}, u32[]{:S(2)}, u32[]{:S(2)}) %collective-permute-start.15) | collective-permute-done | bytes 262176 | tf_op jit(solution)/shard_map/ppermute | solution.py:114
  150.0 3.0 %collective-permute-done.17 = bf16[2,64,512]{2,1,0:T(8,128)(2,1)S(1)} collective-permute-done((bf16[2,64,512]{2,1,0:T(8,128)(2,1)S(1)}, bf16[2,64,512]{2,1,0:T(8,128)(2,1)S(1)}, u32[]{:S(2)}, u32[]{:S(2)}) %collective-permute-start.17) | collective-permute-done | bytes 131104 | tf_op jit(solution)/shard_map/ppermute | solution.py:114
  157.3 3.4 %collective-permute-done.21 = f32[2,32,512]{2,1,0:T(8,128)S(1)} collective-permute-done((f32[2,32,512]{2,1,0:T(8,128)S(1)}, f32[2,32,512]{2,1,0:T(8,128)S(1)}, u32[]{:S(2)}, u32[]{:S(2)}) %collective-permute-start.21) | collective-permute-done | bytes 131104 | tf_op jit(solution)/shard_map/ppermute | solution.py:114
  160.7 2.6 %collective-permute-start.22 = (f32[32,512]{1,0:T(8,128)S(1)}, f32[32,512]{1,0:T(8,128)S(1)}, u32[]{:S(2)}, u32[]{:S(2)}) collective-permute-start(f32[32,512]{1,0:T(8,128)S(1)} %dynamic-slice_bitcast_fusion.4), channel_id=1, source_target_pairs={{0,2},{1,3},{2,0},{3,1},{4,6},{5,7},{6,4},{7,5},{8,10},{9,11},{10,... | collective-permute-start | bytes 196616 | tf_op jit(solution)/shard_map/ppermute | solution.py:114
  166.0 2.7 %collective-permute-start.23 = (f32[32,512]{1,0:T(8,128)S(1)}, f32[32,512]{1,0:T(8,128)S(1)}, u32[]{:S(2)}, u32[]{:S(2)}) collective-permute-start(f32[32,512]{1,0:T(8,128)S(1)} %bitcast_add_fusion.14), channel_id=1, source_target_pairs={{0,2},{1,3},{2,0},{3,1},{4,6},{5,7},{6,4},{7,5},{8,10},{9,11},{10,... | collective-permute-start | bytes 196616 | tf_op jit(solution)/shard_map/ppermute | solution.py:114
  168.7 2.6 %collective-permute-done.23 = f32[32,512]{1,0:T(8,128)S(1)} collective-permute-done((f32[32,512]{1,0:T(8,128)S(1)}, f32[32,512]{1,0:T(8,128)S(1)}, u32[]{:S(2)}, u32[]{:S(2)}) %collective-permute-start.23) | collective-permute-done | bytes 65568 | tf_op jit(solution)/shard_map/ppermute | solution.py:114
  171.4 3.4 %collective-permute-start.24 = (f32[64,512]{1,0:T(8,128)S(1)}, f32[64,512]{1,0:T(8,128)S(1)}, u32[]{:S(2)}, u32[]{:S(2)}) collective-permute-start(f32[64,512]{1,0:T(8,128)S(1)} %pad_maximum_fusion.6), channel_id=1, source_target_pairs={{0,1},{1,0},{2,3},{3,2},{4,5},{5,4},{6,7},{7,6},{8,9},{9,8},{10,11... | collective-permute-start | bytes 393224 | tf_op jit(solution)/shard_map/ppermute | solution.py:114
  174.7 2.9 %collective-permute-done.24 = f32[64,512]{1,0:T(8,128)S(1)} collective-permute-done((f32[64,512]{1,0:T(8,128)S(1)}, f32[64,512]{1,0:T(8,128)S(1)}, u32[]{:S(2)}, u32[]{:S(2)}) %collective-permute-start.24) | collective-permute-done | bytes 131104 | tf_op jit(solution)/shard_map/ppermute | solution.py:114
  178.2 6.0 %collective-permute-done.25 = f32[128,512]{1,0:T(8,128)S(1)} collective-permute-done((f32[128,512]{1,0:T(8,128)S(1)}, f32[128,512]{1,0:T(8,128)S(1)}, u32[]{:S(2)}, u32[]{:S(2)}) %collective-permute-start.25) | collective-permute-done | bytes 262176 | tf_op jit(solution)/shard_map/ppermute | solution.py:114
  205.6 2.9 %collective-permute-done.20 = bf16[64,512]{1,0:T(8,128)(2,1)S(1)} collective-permute-done((bf16[64,512]{1,0:T(8,128)(2,1)S(1)}, bf16[64,512]{1,0:T(8,128)(2,1)S(1)}, u32[]{:S(2)}, u32[]{:S(2)}) %collective-permute-start.20) | collective-permute-done | bytes 65568 | tf_op jit(solution)/shard_map/ppermute | solution.py:114
  211.6 2.9 %div.105 = f32[31,31,512]{2,1,0:T(8,128)} reshape(f32[961,512]{1,0:T(8,128)} %fusion.31) | data formatting | bytes 3936256 | tf_op jit(solution)/shard_map/div | solution.py:262
  (229 shorter events, 105.3 us)
Async XLA Ops:
  4.2 10.2 %collective-permute-start.1 = (bf16[1,15,16,512]{3,2,1,0:T(8,128)(2,1)S(1)}, bf16[1,15,16,512]{3,2,1,0:T(8,128)(2,1)S(1)}, u32[]{:S(2)}, u32[]{:S(2)}) collective-permute-start(bf16[1,15,16,512]{3,2,1,0:T(8,128)(2,1)S(1)} %get-tuple-element.71), channel_id=1, source_target_pairs={{16,0},{17,1},{18,2},{19,3},{20,4},{21,5},{22,6},{23,7},{24,8},{25... | collective-permute-start | bytes 737288 | tf_op jit(solution)/shard_map/ppermute | solution.py:20
  5.5 10.1 %collective-permute-start = (bf16[1,15,16,512]{3,2,1,0:T(8,128)(2,1)S(1)}, bf16[1,15,16,512]{3,2,1,0:T(8,128)(2,1)S(1)}, u32[]{:S(2)}, u32[]{:S(2)}) collective-permute-start(bf16[1,15,16,512]{3,2,1,0:T(8,128)(2,1)S(1)} %get-tuple-element.70), channel_id=1, source_target_pairs={{0,16},{1,17},{2,18},{3,19},{4,20},{5,21},{6,22},{7,23},{8,24},{9,... | collective-permute-start | bytes 737288 | tf_op jit(solution)/shard_map/ppermute | solution.py:19
  18.1 16.7 %collective-permute-start.3 = (bf16[1,46,15,512]{3,1,2,0:T(8,128)(2,1)}, bf16[1,46,15,512]{3,1,2,0:T(8,128)(2,1)}, u32[]{:S(2)}, u32[]{:S(2)}) collective-permute-start(bf16[1,46,15,512]{3,1,2,0:T(8,128)(2,1)} %copy.39), channel_id=1, source_target_pairs={{4,0},{8,4},{12,8},{5,1},{9,5},{13,9},{6,2},{10,6},{14,10},{7,3},{... | collective-permute-start | bytes 2119688 | tf_op jit(solution)/shard_map/ppermute | solution.py:20
  20.7 16.4 %collective-permute-start.2 = (bf16[1,46,15,512]{3,1,2,0:T(8,128)(2,1)}, bf16[1,46,15,512]{3,1,2,0:T(8,128)(2,1)}, u32[]{:S(2)}, u32[]{:S(2)}) collective-permute-start(bf16[1,46,15,512]{3,1,2,0:T(8,128)(2,1)} %copy.38), channel_id=1, source_target_pairs={{0,4},{4,8},{8,12},{1,5},{5,9},{9,13},{2,6},{6,10},{10,14},{3,7},{... | collective-permute-start | bytes 2119688 | tf_op jit(solution)/shard_map/ppermute | solution.py:19
  60.0 24.4 %collective-permute-start.5 = (bf16[1,15,16,512]{3,2,1,0:T(8,128)(2,1)}, bf16[1,15,16,512]{3,2,1,0:T(8,128)(2,1)S(1)}, u32[]{:S(2)}, u32[]{:S(2)}) collective-permute-start(bf16[1,15,16,512]{3,2,1,0:T(8,128)(2,1)} %get-tuple-element.69), channel_id=1, source_target_pairs={{16,0},{17,1},{18,2},{19,3},{20,4},{21,5},{22,6},{23,7},{24,8},{25... | collective-permute-start | bytes 737288 | tf_op jit(solution)/shard_map/ppermute | solution.py:20
  61.3 23.8 %collective-permute-start.4 = (bf16[1,15,16,512]{3,2,1,0:T(8,128)(2,1)S(1)}, bf16[1,15,16,512]{3,2,1,0:T(8,128)(2,1)}, u32[]{:S(2)}, u32[]{:S(2)}) collective-permute-start(bf16[1,15,16,512]{3,2,1,0:T(8,128)(2,1)S(1)} %get-tuple-element.68), channel_id=1, source_target_pairs={{0,16},{1,17},{2,18},{3,19},{4,20},{5,21},{6,22},{7,23},{8,24},{9,... | collective-permute-start | bytes 737288 | tf_op jit(solution)/shard_map/ppermute | solution.py:19
  72.0 15.4 %collective-permute-start.6 = (bf16[2,2,2,2,64,512]{5,4,3,2,1,0:T(8,128)(2,1)}, bf16[2,2,2,2,64,512]{5,4,3,2,1,0:T(8,128)(2,1)}, u32[]{:S(2)}, u32[]{:S(2)}) collective-permute-start(bf16[2,2,2,2,64,512]{5,4,3,2,1,0:T(8,128)(2,1)} %fusion.44), channel_id=1, source_target_pairs={{0,4},{4,0},{8,12},{12,8},{1,5},{5,1},{9,13},{13,9},{2,6},{6,2},{1... | collective-permute-start | bytes 3145736 | tf_op jit(solution)/shard_map/ppermute | solution.py:114
  75.0 14.0 %collective-permute-start.7 = (bf16[2,2,2,2,64,512]{5,4,2,3,1,0:T(8,128)(2,1)S(1)}, bf16[2,2,2,2,64,512]{5,4,2,3,1,0:T(8,128)(2,1)S(1)}, u32[]{:S(2)}, u32[]{:S(2)}) collective-permute-start(bf16[2,2,2,2,64,512]{5,4,2,3,1,0:T(8,128)(2,1)S(1)} %fusion.45), channel_id=1, source_target_pairs={{0,4},{4,0},{8,12},{12,8},{1,5},{5,1},{9,13},{13,9},{2,6},{6,2},{1... | collective-permute-start | bytes 3145736 | tf_op jit(solution)/shard_map/ppermute | solution.py:114
  90.9 22.2 %collective-permute-start.10 = (f32[2,2,2,2,32,512]{5,4,3,2,1,0:T(8,128)}, f32[2,2,2,2,32,512]{5,4,3,2,1,0:T(8,128)}, u32[]{:S(2)}, u32[]{:S(2)}) collective-permute-start(f32[2,2,2,2,32,512]{5,4,3,2,1,0:T(8,128)} %dynamic-slice_bitcast_fusion), channel_id=1, source_target_pairs={{0,4},{4,0},{8,12},{12,8},{1,5},{5,1},{9,13},{13,9},{2,6},{6,2},{1... | collective-permute-start | bytes 3145736 | tf_op jit(solution)/shard_map/ppermute | solution.py:114
  91.0 14.6 %collective-permute-start.11 = (bf16[2,2,2,64,512]{4,3,2,1,0:T(8,128)(2,1)S(1)}, bf16[2,2,2,64,512]{4,3,2,1,0:T(8,128)(2,1)}, u32[]{:S(2)}, u32[]{:S(2)}) collective-permute-start(bf16[2,2,2,64,512]{4,3,2,1,0:T(8,128)(2,1)S(1)} %fusion.62), channel_id=1, source_target_pairs={{0,8},{4,12},{8,0},{12,4},{1,9},{5,13},{9,1},{13,5},{2,10},{6,14},... | collective-permute-start | bytes 1572872 | tf_op jit(solution)/shard_map/ppermute | solution.py:114
  94.1 13.9 %collective-permute-start.12 = (bf16[2,2,2,64,512]{4,3,1,2,0:T(8,128)(2,1)}, bf16[2,2,2,64,512]{4,3,1,2,0:T(8,128)(2,1)}, u32[]{:S(2)}, u32[]{:S(2)}) collective-permute-start(bf16[2,2,2,64,512]{4,3,1,2,0:T(8,128)(2,1)} %fusion.63), channel_id=1, source_target_pairs={{0,16},{16,0},{1,17},{17,1},{2,18},{18,2},{3,19},{19,3},{4,20},{20... | collective-permute-start | bytes 1572872 | tf_op jit(solution)/shard_map/ppermute | solution.py:114
  95.8 13.4 %collective-permute-start.9 = (bf16[1,46,15,512]{3,1,2,0:T(8,128)(2,1)}, bf16[1,46,15,512]{3,1,2,0:T(8,128)(2,1)}, u32[]{:S(2)}, u32[]{:S(2)}) collective-permute-start(bf16[1,46,15,512]{3,1,2,0:T(8,128)(2,1)} %copy.47), channel_id=1, source_target_pairs={{4,0},{8,4},{12,8},{5,1},{9,5},{13,9},{6,2},{10,6},{14,10},{7,3},{... | collective-permute-start | bytes 2119688 | tf_op jit(solution)/shard_map/ppermute | solution.py:20
  98.3 12.4 %collective-permute-start.8 = (bf16[1,46,15,512]{3,1,2,0:T(8,128)(2,1)}, bf16[1,46,15,512]{3,1,2,0:T(8,128)(2,1)}, u32[]{:S(2)}, u32[]{:S(2)}) collective-permute-start(bf16[1,46,15,512]{3,1,2,0:T(8,128)(2,1)} %copy.46), channel_id=1, source_target_pairs={{0,4},{4,8},{8,12},{1,5},{5,9},{9,13},{2,6},{6,10},{10,14},{3,7},{... | collective-permute-start | bytes 2119688 | tf_op jit(solution)/shard_map/ppermute | solution.py:19
  123.6 22.3 %collective-permute-start.13 = (f32[2,2,2,32,512]{4,3,2,1,0:T(8,128)S(1)}, f32[2,2,2,32,512]{4,3,2,1,0:T(8,128)S(1)}, u32[]{:S(2)}, u32[]{:S(2)}) collective-permute-start(f32[2,2,2,32,512]{4,3,2,1,0:T(8,128)S(1)} %dynamic-slice_bitcast_fusion.1), channel_id=1, source_target_pairs={{0,8},{4,12},{8,0},{12,4},{1,9},{5,13},{9,1},{13,5},{2,10},{6,14},... | collective-permute-start | bytes 1572872 | tf_op jit(solution)/shard_map/ppermute | solution.py:114
  128.1 7.9 %collective-permute-start.14 = (bf16[2,2,64,512]{3,2,1,0:T(8,128)(2,1)S(1)}, bf16[2,2,64,512]{3,2,1,0:T(8,128)(2,1)S(1)}, u32[]{:S(2)}, u32[]{:S(2)}) collective-permute-start(bf16[2,2,64,512]{3,2,1,0:T(8,128)(2,1)S(1)} %fusion.65), channel_id=1, source_target_pairs={{0,16},{16,0},{1,17},{17,1},{2,18},{18,2},{3,19},{19,3},{4,20},{20... | collective-permute-start | bytes 786440 | tf_op jit(solution)/shard_map/ppermute | solution.py:114
  128.2 17.6 %collective-permute-start.15 = (bf16[2,2,64,512]{3,2,0,1:T(8,128)(2,1)S(1)}, bf16[2,2,64,512]{3,2,0,1:T(8,128)(2,1)S(1)}, u32[]{:S(2)}, u32[]{:S(2)}) collective-permute-start(bf16[2,2,64,512]{3,2,0,1:T(8,128)(2,1)S(1)} %fusion.66), channel_id=1, source_target_pairs={{0,8},{4,12},{8,0},{12,4},{1,9},{5,13},{9,1},{13,5},{2,10},{6,14},... | collective-permute-start | bytes 786440 | tf_op jit(solution)/shard_map/ppermute | solution.py:114
  146.0 9.6 %collective-permute-start.16 = (f32[2,2,32,512]{3,2,1,0:T(8,128)S(1)}, f32[2,2,32,512]{3,2,1,0:T(8,128)S(1)}, u32[]{:S(2)}, u32[]{:S(2)}) collective-permute-start(f32[2,2,32,512]{3,2,1,0:T(8,128)S(1)} %dynamic-slice_bitcast_fusion.2), channel_id=1, source_target_pairs={{0,16},{16,0},{1,17},{17,1},{2,18},{18,2},{3,19},{19,3},{4,20},{20... | collective-permute-start | bytes 786440 | tf_op jit(solution)/shard_map/ppermute | solution.py:114
  146.6 6.4 %collective-permute-start.17 = (bf16[2,64,512]{2,1,0:T(8,128)(2,1)S(1)}, bf16[2,64,512]{2,1,0:T(8,128)(2,1)S(1)}, u32[]{:S(2)}, u32[]{:S(2)}) collective-permute-start(bf16[2,64,512]{2,1,0:T(8,128)(2,1)S(1)} %fusion.67), channel_id=1, source_target_pairs={{0,1},{1,0},{2,3},{3,2},{4,5},{5,4},{6,7},{7,6},{8,9},{9,8},{10,11... | collective-permute-start | bytes 393224 | tf_op jit(solution)/shard_map/ppermute | solution.py:114
  148.3 6.6 %collective-permute-start.18 = (bf16[2,64,512]{2,1,0:T(8,128)(2,1)S(1)}, bf16[2,64,512]{2,1,0:T(8,128)(2,1)S(1)}, u32[]{:S(2)}, u32[]{:S(2)}) collective-permute-start(bf16[2,64,512]{2,1,0:T(8,128)(2,1)S(1)} %fusion.68), channel_id=1, source_target_pairs={{0,1},{1,0},{2,3},{3,2},{4,5},{5,4},{6,7},{7,6},{8,9},{9,8},{10,11... | collective-permute-start | bytes 393224 | tf_op jit(solution)/shard_map/ppermute | solution.py:114
  177.7 6.4 %collective-permute-start.25 = (f32[128,512]{1,0:T(8,128)S(1)}, f32[128,512]{1,0:T(8,128)S(1)}, u32[]{:S(2)}, u32[]{:S(2)}) collective-permute-start(f32[128,512]{1,0:T(8,128)S(1)} %pad_maximum_fusion.5), channel_id=1, source_target_pairs={{0,16},{16,0},{1,17},{17,1},{2,18},{18,2},{3,19},{19,3},{4,20},{20... | collective-permute-start | bytes 786440 | tf_op jit(solution)/shard_map/ppermute | solution.py:114
  184.3 11.2 %collective-permute-start.26 = (f32[256,512]{1,0:T(8,128)S(1)}, f32[256,512]{1,0:T(8,128)}, u32[]{:S(2)}, u32[]{:S(2)}) collective-permute-start(f32[256,512]{1,0:T(8,128)S(1)} %pad_maximum_fusion.4), channel_id=1, source_target_pairs={{0,8},{4,12},{8,0},{12,4},{1,9},{5,13},{9,1},{13,5},{2,10},{6,14},... | collective-permute-start | bytes 1572872 | tf_op jit(solution)/shard_map/ppermute | solution.py:114
  196.8 12.4 %collective-permute-start.27 = (f32[512,512]{1,0:T(8,128)S(1)}, f32[512,512]{1,0:T(8,128)S(1)}, u32[]{:S(2)}, u32[]{:S(2)}) collective-permute-start(f32[512,512]{1,0:T(8,128)S(1)} %pad_maximum_fusion.1), channel_id=1, source_target_pairs={{0,4},{4,0},{8,12},{12,8},{1,5},{5,1},{9,13},{13,9},{2,6},{6,2},{1... | collective-permute-start | bytes 3145736 | tf_op jit(solution)/shard_map/ppermute | solution.py:114
  198.2 6.8 %collective-permute-start.19 = (bf16[64,512]{1,0:T(8,128)(2,1)S(1)}, bf16[64,512]{1,0:T(8,128)(2,1)S(1)}, u32[]{:S(2)}, u32[]{:S(2)}) collective-permute-start(bf16[64,512]{1,0:T(8,128)(2,1)S(1)} %fusion.71), channel_id=1, source_target_pairs={{0,2},{1,3},{2,0},{3,1},{4,6},{5,7},{6,4},{7,5},{8,10},{9,11},{10,... | collective-permute-start | bytes 196616 | tf_op jit(solution)/shard_map/ppermute | solution.py:114
  201.7 6.9 %collective-permute-start.20 = (bf16[64,512]{1,0:T(8,128)(2,1)S(1)}, bf16[64,512]{1,0:T(8,128)(2,1)S(1)}, u32[]{:S(2)}, u32[]{:S(2)}) collective-permute-start(bf16[64,512]{1,0:T(8,128)(2,1)S(1)} %fusion.72), channel_id=1, source_target_pairs={{0,2},{1,3},{2,0},{3,1},{4,6},{5,7},{6,4},{7,5},{8,10},{9,11},{10,... | collective-permute-start | bytes 196616 | tf_op jit(solution)/shard_map/ppermute | solution.py:114
  (49 other events, 302.9 us)

commit v4 on v3

--- a/solution.py
+++ b/solution.py
@@ -246,14 +246,22 @@
     gain_first_sum = jnp.sum(grad_source * normed_first, axis=(0, 1, 2))[None]
     gain_first_sum, small, up_sum, down_sum = fence((gain_first_sum, small, up_sum, down_sum))
 
-    for step in range(4, steps):
-        up_sum = up_step(up_sum, step)
-        down_sum = down_step(down_sum, step)
+    rest = [pair for pair in reversed(columns_next)]
+    summed = 0
     for step in range(3, steps):
         small = halve(small, columns_next, columns_next, step, jnp.float32)
-    for axis, bit in reversed(columns_next):
+        up_sum = up_step(up_sum, step + 1)
+        down_sum = down_step(down_sum, step + 1)
+        if step > 3 or steps < 5:
+            gain_first_sum = gain_first_sum + swap(gain_first_sum, *rest[summed])
+            summed += 1
+        small, gain_first_sum, up_sum, down_sum = fence((small, gain_first_sum, up_sum, down_sum))
+    for axis, bit in rest:
         small = double(small, axis, bit)
-        gain_first_sum = gain_first_sum + swap(gain_first_sum, axis, bit)
+        if summed < steps:
+            gain_first_sum = gain_first_sum + swap(gain_first_sum, *rest[summed])
+            summed += 1
+        small, gain_first_sum = fence((small, gain_first_sum))
     divisor = tile_rows * lax.axis_size("gy")
     return (
         grad_input,

time: 215 us -> 211 us (0.981)
  starting transfers between devices: 56.5 us -> 50.9 us
    ppermute x25, starting transfers between devices: 33.4 us -> 27.7 us  [swap(): return lax.ppermute(values, axis, [(i, i ^ bit) for i in range(size)])]
    add x13 -> x15, other arithmetic: 7.91 us -> 6.57 us  [halve(): return kept + swap(sent, axis, bit).astype(jnp.float32)]
    unnamed x80 -> x76, local copies, waits for them, and re-layouts: 8.38 us -> 9.7 us
  transfers between devices with their start and end apart: 33 -> 33, of which waited for: 18 -> 19; matrix products, arithmetic and copies ran while one was open for 23% -> 22% of each run, Pallas kernels for 0% -> 0%
where the time goes in v4:
time: 211 us; the launch traced here: 210 us
  waiting for transfers between devices  56.8 us (27%)
  starting transfers between devices  50.9 us (24%)
  matrix products  39.6 us (19%)
  local copies, waits for them, and re-layouts  34.4 us (16%)
  other arithmetic  26.4 us (13%)
    ppermute x25, waiting for transfers between devices, swap(): return lax.ppermute(values, axis, [(i, i ^ bit) for i in range(size)])  51.6 us
    ppermute x25, starting transfers between devices, swap(): return lax.ppermute(values, axis, [(i, i ^ bit) for i in range(size)])  27.7 us
    dot_general x4, matrix products, forward_transform(): jnp.einsum('fp,bpc->bfc', table, values, preferred_element_type=jnp.float32)  21.9 us
    ppermute x4, starting transfers between devices, padded_2(): before = lax.ppermute(last, axis, up)  18 us
    unnamed x76, local copies, waits for them, and re-layouts  9.7 us
    dot_general x5, matrix products, inverse_transform(): jnp.einsum('fp,bfc->bpc', table, spectrum, preferred_element_type=jnp.flo...  9.39 us
    add x15, other arithmetic, halve(): return kept + swap(sent, axis, bit).astype(jnp.float32)  6.57 us
    ppermute x4, starting transfers between devices, padded_2(): after = lax.ppermute(initial, axis, down)  5.13 us
  transfers between devices with their start and end apart: 33, of which 19 were waited for; matrix products, arithmetic and copies ran while one was open for 22% of the time, Pallas kernels for 0%

profile of v4, /device:TPU:0, one launch (start us, length us, event | category | flops | bytes accessed | tf_op | source)
XLA Modules:
  0.0 209.8 jit_solution(16621537230850419118)
XLA Ops:
  5.5 4.9 %collective-permute-start = (bf16[1,15,16,512]{3,2,1,0:T(8,128)(2,1)S(1)}, bf16[1,15,16,512]{3,2,1,0:T(8,128)(2,1)S(1)}, u32[]{:S(2)}, u32[]{:S(2)}) collective-permute-start(bf16[1,15,16,512]{3,2,1,0:T(8,128)(2,1)S(1)} %get-tuple-element.106), channel_id=1, source_target_pairs={{0,16},{1,17},{2,18},{3,19},{4,20},{5,21},{6,22},{7,23},{8,24},{9,... | collective-permute-start | bytes 737288 | tf_op jit(solution)/shard_map/ppermute | solution.py:19
  10.4 4.0 %collective-permute-done.1 = bf16[1,15,16,512]{3,2,1,0:T(8,128)(2,1)S(1)} collective-permute-done((bf16[1,15,16,512]{3,2,1,0:T(8,128)(2,1)S(1)}, bf16[1,15,16,512]{3,2,1,0:T(8,128)(2,1)S(1)}, u32[]{:S(2)}, u32[]{:S(2)}) %collective-permute-start.1) | collective-permute-done | bytes 245792 | tf_op jit(solution)/shard_map/ppermute | solution.py:20
  20.7 3.9 %collective-permute-start.2 = (bf16[1,46,15,512]{3,1,2,0:T(8,128)(2,1)}, bf16[1,46,15,512]{3,1,2,0:T(8,128)(2,1)}, u32[]{:S(2)}, u32[]{:S(2)}) collective-permute-start(bf16[1,46,15,512]{3,1,2,0:T(8,128)(2,1)} %copy.38), channel_id=1, source_target_pairs={{0,4},{4,8},{8,12},{1,5},{5,9},{9,13},{2,6},{6,10},{10,14},{3,7},{... | collective-permute-start | bytes 2119688 | tf_op jit(solution)/shard_map/ppermute | solution.py:19
  29.8 5.0 %convolution_bitcast_fusion.3 = f32[1,2120,512]{2,1,0:T(8,128)S(1)} fusion(bf16[2120,961]{1,0:T(8,128)(2,1)} %constant.281.clone, bf16[961,512]{1,0:T(8,128)(2,1)} %convert_element_type.148), kind=kOutput, calls=%fused_computation.3 | convolution fusion | flops 2086215680 | bytes 9400464 | tf_op jit(solution)/shard_map/fp,bpc->bfc/dot_general | solution.py:88
  40.1 7.9 %convolution_bitcast_fusion.1 = f32[1,2120,512]{2,1,0:T(8,128)S(1)} fusion(bf16[2208,512]{1,0:T(8,128)(2,1)S(1)} %bitcast.191, bf16[2120,2208]{1,0:T(8,128)(2,1)} %constant.278.clone), kind=kOutput, calls=%fused_computation.1 | convolution fusion | flops 4793303040 | bytes 15964672 | tf_op jit(solution)/shard_map/fp,bpc->bfc/dot_general | solution.py:88
  52.8 3.2 %multiply_convert_fusion.6 = (bf16[2048,256]{0,1:T(8,128)(2,1)}, bf16[2048,256]{0,1:T(8,128)(2,1)}, f32[256,2048]{1,0:T(8,128)S(1)}) fusion(f32[256,2048]{1,0:T(8,128)S(1)} %copy-done.16, bf16[256,512]{1,0:T(8,128)(2,1)S(1)} %bitcast.192, bf16[512,2048]{1,0:T(8,128)(2,1)S(1)} %copy-done), kind=kOutput, calls=%fused_computation.53 | convolution fusion | flops 547880960 | bytes 8650752 | tf_op jit(solution)/shard_map/dot_general | solution.py:159
  61.4 5.3 %collective-permute-start.4 = (bf16[1,15,16,512]{3,2,1,0:T(8,128)(2,1)S(1)}, bf16[1,15,16,512]{3,2,1,0:T(8,128)(2,1)}, u32[]{:S(2)}, u32[]{:S(2)}) collective-permute-start(bf16[1,15,16,512]{3,2,1,0:T(8,128)(2,1)S(1)} %get-tuple-element.104), channel_id=1, source_target_pairs={{0,16},{1,17},{2,18},{3,19},{4,20},{5,21},{6,22},{7,23},{8,24},{9,... | collective-permute-start | bytes 737288 | tf_op jit(solution)/shard_map/ppermute | solution.py:19
  77.8 4.5 %fusion.39 = f32[512,961]{0,1:T(8,128)S(1)} fusion(bf16[1060,961]{1,0:T(8,128)(2,1)S(1)} %copy-done.29, f32[1,2120,512]{2,1,0:T(8,128)S(1)} %convolution_bitcast_fusion.2, f32[1,2120,512]{2,1,0:T(8,128)} %copy-done.33, f32[1060]{0:T(1024)S(1)} %copy-done.27), kind=kOutput, calls=%fused_computation.64 | convolution fusion | flops 1045821440 | bytes 12871680 | tf_op jit(solution)/shard_map/fp,bfc->bpc/dot_general | solution.py:95
  98.4 3.9 %collective-permute-start.8 = (bf16[1,46,15,512]{3,1,2,0:T(8,128)(2,1)}, bf16[1,46,15,512]{3,1,2,0:T(8,128)(2,1)}, u32[]{:S(2)}, u32[]{:S(2)}) collective-permute-start(bf16[1,46,15,512]{3,1,2,0:T(8,128)(2,1)} %copy.46), channel_id=1, source_target_pairs={{0,4},{4,8},{8,12},{1,5},{5,9},{9,13},{2,6},{6,10},{10,14},{3,7},{... | collective-permute-start | bytes 2119688 | tf_op jit(solution)/shard_map/ppermute | solution.py:19
  102.3 3.3 %collective-permute-done.11 = bf16[2,2,2,64,512]{4,3,2,1,0:T(8,128)(2,1)} collective-permute-done((bf16[2,2,2,64,512]{4,3,2,1,0:T(8,128)(2,1)S(1)}, bf16[2,2,2,64,512]{4,3,2,1,0:T(8,128)(2,1)}, u32[]{:S(2)}, u32[]{:S(2)}) %collective-permute-start.11) | collective-permute-done | bytes 524320 | tf_op jit(solution)/shard_map/ppermute | solution.py:114
  115.4 8.3 %convolution_bitcast_fusion = f32[1,2120,512]{2,1,0:T(8,128)S(1)} fusion(bf16[2208,512]{1,0:T(8,128)(2,1)S(1)} %bitcast.190, bf16[2120,2208]{1,0:T(8,128)(2,1)} %constant.278.clone), kind=kOutput, calls=%fused_computation | convolution fusion | flops 4793303040 | bytes 15964672 | tf_op jit(solution)/shard_map/fp,bpc->bfc/dot_general | solution.py:88
  123.7 4.4 %collective-permute-start.13 = (f32[2,2,2,32,512]{4,3,2,1,0:T(8,128)S(1)}, f32[2,2,2,32,512]{4,3,2,1,0:T(8,128)S(1)}, u32[]{:S(2)}, u32[]{:S(2)}) collective-permute-start(f32[2,2,2,32,512]{4,3,2,1,0:T(8,128)S(1)} %dynamic-slice_bitcast_fusion.1), channel_id=1, source_target_pairs={{0,8},{4,12},{8,0},{12,4},{1,9},{5,13},{9,1},{13,5},{2,10},{6,14},... | collective-permute-start | bytes 1572872 | tf_op jit(solution)/shard_map/ppermute | solution.py:114
  129.4 6.7 %collective-permute-done.14 = bf16[2,2,64,512]{3,2,1,0:T(8,128)(2,1)S(1)} collective-permute-done((bf16[2,2,64,512]{3,2,1,0:T(8,128)(2,1)S(1)}, bf16[2,2,64,512]{3,2,1,0:T(8,128)(2,1)S(1)}, u32[]{:S(2)}, u32[]{:S(2)}) %collective-permute-start.14) | collective-permute-done | bytes 262176 | tf_op jit(solution)/shard_map/ppermute | solution.py:114
  136.2 9.6 %collective-permute-done.15 = bf16[2,2,64,512]{3,2,0,1:T(8,128)(2,1)S(1)} collective-permute-done((bf16[2,2,64,512]{3,2,0,1:T(8,128)(2,1)S(1)}, bf16[2,2,64,512]{3,2,0,1:T(8,128)(2,1)S(1)}, u32[]{:S(2)}, u32[]{:S(2)}) %collective-permute-start.15) | collective-permute-done | bytes 262176 | tf_op jit(solution)/shard_map/ppermute | solution.py:114
  150.1 3.0 %collective-permute-done.17 = bf16[2,64,512]{2,1,0:T(8,128)(2,1)S(1)} collective-permute-done((bf16[2,64,512]{2,1,0:T(8,128)(2,1)S(1)}, bf16[2,64,512]{2,1,0:T(8,128)(2,1)S(1)}, u32[]{:S(2)}, u32[]{:S(2)}) %collective-permute-start.17) | collective-permute-done | bytes 131104 | tf_op jit(solution)/shard_map/ppermute | solution.py:114
  156.7 2.7 %collective-permute-start.20 = (bf16[64,512]{1,0:T(8,128)(2,1)S(1)}, bf16[64,512]{1,0:T(8,128)(2,1)S(1)}, u32[]{:S(2)}, u32[]{:S(2)}) collective-permute-start(bf16[64,512]{1,0:T(8,128)(2,1)S(1)} %fusion.68), channel_id=1, source_target_pairs={{0,2},{1,3},{2,0},{3,1},{4,6},{5,7},{6,4},{7,5},{8,10},{9,11},{10,... | collective-permute-start | bytes 196616 | tf_op jit(solution)/shard_map/ppermute | solution.py:114
  159.7 3.5 %collective-permute-done.20 = bf16[64,512]{1,0:T(8,128)(2,1)S(1)} collective-permute-done((bf16[64,512]{1,0:T(8,128)(2,1)S(1)}, bf16[64,512]{1,0:T(8,128)(2,1)S(1)}, u32[]{:S(2)}, u32[]{:S(2)}) %collective-permute-start.20) | collective-permute-done | bytes 65568 | tf_op jit(solution)/shard_map/ppermute | solution.py:114
  163.2 2.7 %collective-permute-done.21 = bf16[64,512]{1,0:T(8,128)(2,1)S(1)} collective-permute-done((bf16[64,512]{1,0:T(8,128)(2,1)S(1)}, bf16[64,512]{1,0:T(8,128)(2,1)S(1)}, u32[]{:S(2)}, u32[]{:S(2)}) %collective-permute-start.21) | collective-permute-done | bytes 65568 | tf_op jit(solution)/shard_map/ppermute | solution.py:114
  166.1 2.9 %collective-permute-start.23 = (f32[1,512]{1,0:T(1,128)S(1)}, f32[1,512]{1,0:T(1,128)S(1)}, u32[]{:S(2)}, u32[]{:S(2)}) collective-permute-start(f32[1,512]{1,0:T(1,128)S(1)} %bitcast.196), channel_id=1, source_target_pairs={{0,2},{1,3},{2,0},{3,1},{4,6},{5,7},{6,4},{7,5},{8,10},{9,11},{10,... | collective-permute-start | bytes 6152 | tf_op jit(solution)/shard_map/ppermute | solution.py:114
  171.3 2.3 %collective-permute-start.24 = (f32[32,512]{1,0:T(8,128)S(1)}, f32[32,512]{1,0:T(8,128)S(1)}, u32[]{:S(2)}, u32[]{:S(2)}) collective-permute-start(f32[32,512]{1,0:T(8,128)S(1)} %bitcast_add_fusion.14), channel_id=1, source_target_pairs={{0,2},{1,3},{2,0},{3,1},{4,6},{5,7},{6,4},{7,5},{8,10},{9,11},{10,... | collective-permute-start | bytes 196616 | tf_op jit(solution)/shard_map/ppermute | solution.py:114
  173.8 3.4 %collective-permute-done.25 = f32[1,512]{1,0:T(1,128)S(1)} collective-permute-done((f32[1,512]{1,0:T(1,128)S(1)}, f32[1,512]{1,0:T(1,128)S(1)}, u32[]{:S(2)}, u32[]{:S(2)}) %collective-permute-start.25) | collective-permute-done | bytes 2080 | tf_op jit(solution)/shard_map/ppermute | solution.py:114
  185.2 2.6 %collective-permute-done.29 = f32[1,512]{1,0:T(1,128)S(1)} collective-permute-done((f32[1,512]{1,0:T(1,128)S(1)}, f32[1,512]{1,0:T(1,128)S(1)}, u32[]{:S(2)}, u32[]{:S(2)}) %collective-permute-start.29) | collective-permute-done | bytes 2080 | tf_op jit(solution)/shard_map/ppermute | solution.py:114
  191.4 6.7 %collective-permute-done.30 = f32[256,512]{1,0:T(8,128)S(1)} collective-permute-done((f32[256,512]{1,0:T(8,128)S(1)}, f32[256,512]{1,0:T(8,128)S(1)}, u32[]{:S(2)}, u32[]{:S(2)}) %collective-permute-start.30) | collective-permute-done | bytes 524320 | tf_op jit(solution)/shard_map/ppermute | solution.py:114
  205.6 2.9 %div.105 = f32[31,31,512]{2,1,0:T(8,128)} reshape(f32[961,512]{1,0:T(8,128)} %slice_multiply_fusion) | data formatting | bytes 3936256 | tf_op jit(solution)/shard_map/div | solution.py:270
  (227 shorter events, 100.7 us)
Async XLA Ops:
  4.2 10.2 %collective-permute-start.1 = (bf16[1,15,16,512]{3,2,1,0:T(8,128)(2,1)S(1)}, bf16[1,15,16,512]{3,2,1,0:T(8,128)(2,1)S(1)}, u32[]{:S(2)}, u32[]{:S(2)}) collective-permute-start(bf16[1,15,16,512]{3,2,1,0:T(8,128)(2,1)S(1)} %get-tuple-element.107), channel_id=1, source_target_pairs={{16,0},{17,1},{18,2},{19,3},{20,4},{21,5},{22,6},{23,7},{24,8},{25... | collective-permute-start | bytes 737288 | tf_op jit(solution)/shard_map/ppermute | solution.py:20
  5.5 10.1 %collective-permute-start = (bf16[1,15,16,512]{3,2,1,0:T(8,128)(2,1)S(1)}, bf16[1,15,16,512]{3,2,1,0:T(8,128)(2,1)S(1)}, u32[]{:S(2)}, u32[]{:S(2)}) collective-permute-start(bf16[1,15,16,512]{3,2,1,0:T(8,128)(2,1)S(1)} %get-tuple-element.106), channel_id=1, source_target_pairs={{0,16},{1,17},{2,18},{3,19},{4,20},{5,21},{6,22},{7,23},{8,24},{9,... | collective-permute-start | bytes 737288 | tf_op jit(solution)/shard_map/ppermute | solution.py:19
  18.1 16.7 %collective-permute-start.3 = (bf16[1,46,15,512]{3,1,2,0:T(8,128)(2,1)}, bf16[1,46,15,512]{3,1,2,0:T(8,128)(2,1)}, u32[]{:S(2)}, u32[]{:S(2)}) collective-permute-start(bf16[1,46,15,512]{3,1,2,0:T(8,128)(2,1)} %copy.39), channel_id=1, source_target_pairs={{4,0},{8,4},{12,8},{5,1},{9,5},{13,9},{6,2},{10,6},{14,10},{7,3},{... | collective-permute-start | bytes 2119688 | tf_op jit(solution)/shard_map/ppermute | solution.py:20
  20.7 16.4 %collective-permute-start.2 = (bf16[1,46,15,512]{3,1,2,0:T(8,128)(2,1)}, bf16[1,46,15,512]{3,1,2,0:T(8,128)(2,1)}, u32[]{:S(2)}, u32[]{:S(2)}) collective-permute-start(bf16[1,46,15,512]{3,1,2,0:T(8,128)(2,1)} %copy.38), channel_id=1, source_target_pairs={{0,4},{4,8},{8,12},{1,5},{5,9},{9,13},{2,6},{6,10},{10,14},{3,7},{... | collective-permute-start | bytes 2119688 | tf_op jit(solution)/shard_map/ppermute | solution.py:19
  60.1 24.4 %collective-permute-start.5 = (bf16[1,15,16,512]{3,2,1,0:T(8,128)(2,1)}, bf16[1,15,16,512]{3,2,1,0:T(8,128)(2,1)S(1)}, u32[]{:S(2)}, u32[]{:S(2)}) collective-permute-start(bf16[1,15,16,512]{3,2,1,0:T(8,128)(2,1)} %get-tuple-element.105), channel_id=1, source_target_pairs={{16,0},{17,1},{18,2},{19,3},{20,4},{21,5},{22,6},{23,7},{24,8},{25... | collective-permute-start | bytes 737288 | tf_op jit(solution)/shard_map/ppermute | solution.py:20
  61.4 23.8 %collective-permute-start.4 = (bf16[1,15,16,512]{3,2,1,0:T(8,128)(2,1)S(1)}, bf16[1,15,16,512]{3,2,1,0:T(8,128)(2,1)}, u32[]{:S(2)}, u32[]{:S(2)}) collective-permute-start(bf16[1,15,16,512]{3,2,1,0:T(8,128)(2,1)S(1)} %get-tuple-element.104), channel_id=1, source_target_pairs={{0,16},{1,17},{2,18},{3,19},{4,20},{5,21},{6,22},{7,23},{8,24},{9,... | collective-permute-start | bytes 737288 | tf_op jit(solution)/shard_map/ppermute | solution.py:19
  72.1 15.4 %collective-permute-start.6 = (bf16[2,2,2,2,64,512]{5,4,3,2,1,0:T(8,128)(2,1)}, bf16[2,2,2,2,64,512]{5,4,3,2,1,0:T(8,128)(2,1)}, u32[]{:S(2)}, u32[]{:S(2)}) collective-permute-start(bf16[2,2,2,2,64,512]{5,4,3,2,1,0:T(8,128)(2,1)} %fusion.43), channel_id=1, source_target_pairs={{0,4},{4,0},{8,12},{12,8},{1,5},{5,1},{9,13},{13,9},{2,6},{6,2},{1... | collective-permute-start | bytes 3145736 | tf_op jit(solution)/shard_map/ppermute | solution.py:114
  75.1 14.0 %collective-permute-start.7 = (bf16[2,2,2,2,64,512]{5,4,2,3,1,0:T(8,128)(2,1)S(1)}, bf16[2,2,2,2,64,512]{5,4,2,3,1,0:T(8,128)(2,1)S(1)}, u32[]{:S(2)}, u32[]{:S(2)}) collective-permute-start(bf16[2,2,2,2,64,512]{5,4,2,3,1,0:T(8,128)(2,1)S(1)} %fusion.44), channel_id=1, source_target_pairs={{0,4},{4,0},{8,12},{12,8},{1,5},{5,1},{9,13},{13,9},{2,6},{6,2},{1... | collective-permute-start | bytes 3145736 | tf_op jit(solution)/shard_map/ppermute | solution.py:114
  90.9 22.2 %collective-permute-start.10 = (f32[2,2,2,2,32,512]{5,4,3,2,1,0:T(8,128)}, f32[2,2,2,2,32,512]{5,4,3,2,1,0:T(8,128)}, u32[]{:S(2)}, u32[]{:S(2)}) collective-permute-start(f32[2,2,2,2,32,512]{5,4,3,2,1,0:T(8,128)} %dynamic-slice_bitcast_fusion), channel_id=1, source_target_pairs={{0,4},{4,0},{8,12},{12,8},{1,5},{5,1},{9,13},{13,9},{2,6},{6,2},{1... | collective-permute-start | bytes 3145736 | tf_op jit(solution)/shard_map/ppermute | solution.py:114
  91.0 14.6 %collective-permute-start.11 = (bf16[2,2,2,64,512]{4,3,2,1,0:T(8,128)(2,1)S(1)}, bf16[2,2,2,64,512]{4,3,2,1,0:T(8,128)(2,1)}, u32[]{:S(2)}, u32[]{:S(2)}) collective-permute-start(bf16[2,2,2,64,512]{4,3,2,1,0:T(8,128)(2,1)S(1)} %fusion.61), channel_id=1, source_target_pairs={{0,8},{4,12},{8,0},{12,4},{1,9},{5,13},{9,1},{13,5},{2,10},{6,14},... | collective-permute-start | bytes 1572872 | tf_op jit(solution)/shard_map/ppermute | solution.py:114
  94.2 13.9 %collective-permute-start.12 = (bf16[2,2,2,64,512]{4,3,1,2,0:T(8,128)(2,1)}, bf16[2,2,2,64,512]{4,3,1,2,0:T(8,128)(2,1)}, u32[]{:S(2)}, u32[]{:S(2)}) collective-permute-start(bf16[2,2,2,64,512]{4,3,1,2,0:T(8,128)(2,1)} %fusion.62), channel_id=1, source_target_pairs={{0,16},{16,0},{1,17},{17,1},{2,18},{18,2},{3,19},{19,3},{4,20},{20... | collective-permute-start | bytes 1572872 | tf_op jit(solution)/shard_map/ppermute | solution.py:114
  95.8 13.4 %collective-permute-start.9 = (bf16[1,46,15,512]{3,1,2,0:T(8,128)(2,1)}, bf16[1,46,15,512]{3,1,2,0:T(8,128)(2,1)}, u32[]{:S(2)}, u32[]{:S(2)}) collective-permute-start(bf16[1,46,15,512]{3,1,2,0:T(8,128)(2,1)} %copy.47), channel_id=1, source_target_pairs={{4,0},{8,4},{12,8},{5,1},{9,5},{13,9},{6,2},{10,6},{14,10},{7,3},{... | collective-permute-start | bytes 2119688 | tf_op jit(solution)/shard_map/ppermute | solution.py:20
  98.4 12.4 %collective-permute-start.8 = (bf16[1,46,15,512]{3,1,2,0:T(8,128)(2,1)}, bf16[1,46,15,512]{3,1,2,0:T(8,128)(2,1)}, u32[]{:S(2)}, u32[]{:S(2)}) collective-permute-start(bf16[1,46,15,512]{3,1,2,0:T(8,128)(2,1)} %copy.46), channel_id=1, source_target_pairs={{0,4},{4,8},{8,12},{1,5},{5,9},{9,13},{2,6},{6,10},{10,14},{3,7},{... | collective-permute-start | bytes 2119688 | tf_op jit(solution)/shard_map/ppermute | solution.py:19
  123.7 22.2 %collective-permute-start.13 = (f32[2,2,2,32,512]{4,3,2,1,0:T(8,128)S(1)}, f32[2,2,2,32,512]{4,3,2,1,0:T(8,128)S(1)}, u32[]{:S(2)}, u32[]{:S(2)}) collective-permute-start(f32[2,2,2,32,512]{4,3,2,1,0:T(8,128)S(1)} %dynamic-slice_bitcast_fusion.1), channel_id=1, source_target_pairs={{0,8},{4,12},{8,0},{12,4},{1,9},{5,13},{9,1},{13,5},{2,10},{6,14},... | collective-permute-start | bytes 1572872 | tf_op jit(solution)/shard_map/ppermute | solution.py:114
  128.1 8.0 %collective-permute-start.14 = (bf16[2,2,64,512]{3,2,1,0:T(8,128)(2,1)S(1)}, bf16[2,2,64,512]{3,2,1,0:T(8,128)(2,1)S(1)}, u32[]{:S(2)}, u32[]{:S(2)}) collective-permute-start(bf16[2,2,64,512]{3,2,1,0:T(8,128)(2,1)S(1)} %fusion.64), channel_id=1, source_target_pairs={{0,16},{16,0},{1,17},{17,1},{2,18},{18,2},{3,19},{19,3},{4,20},{20... | collective-permute-start | bytes 786440 | tf_op jit(solution)/shard_map/ppermute | solution.py:114
  128.3 17.5 %collective-permute-start.15 = (bf16[2,2,64,512]{3,2,0,1:T(8,128)(2,1)S(1)}, bf16[2,2,64,512]{3,2,0,1:T(8,128)(2,1)S(1)}, u32[]{:S(2)}, u32[]{:S(2)}) collective-permute-start(bf16[2,2,64,512]{3,2,0,1:T(8,128)(2,1)S(1)} %fusion.65), channel_id=1, source_target_pairs={{0,8},{4,12},{8,0},{12,4},{1,9},{5,13},{9,1},{13,5},{2,10},{6,14},... | collective-permute-start | bytes 786440 | tf_op jit(solution)/shard_map/ppermute | solution.py:114
  146.0 8.9 %collective-permute-start.16 = (f32[2,2,32,512]{3,2,1,0:T(8,128)S(1)}, f32[2,2,32,512]{3,2,1,0:T(8,128)S(1)}, u32[]{:S(2)}, u32[]{:S(2)}) collective-permute-start(f32[2,2,32,512]{3,2,1,0:T(8,128)S(1)} %dynamic-slice_bitcast_fusion.2), channel_id=1, source_target_pairs={{0,16},{16,0},{1,17},{17,1},{2,18},{18,2},{3,19},{19,3},{4,20},{20... | collective-permute-start | bytes 786440 | tf_op jit(solution)/shard_map/ppermute | solution.py:114
  146.7 6.4 %collective-permute-start.17 = (bf16[2,64,512]{2,1,0:T(8,128)(2,1)S(1)}, bf16[2,64,512]{2,1,0:T(8,128)(2,1)S(1)}, u32[]{:S(2)}, u32[]{:S(2)}) collective-permute-start(bf16[2,64,512]{2,1,0:T(8,128)(2,1)S(1)} %fusion.66), channel_id=1, source_target_pairs={{0,1},{1,0},{2,3},{3,2},{4,5},{5,4},{6,7},{7,6},{8,9},{9,8},{10,11... | collective-permute-start | bytes 393224 | tf_op jit(solution)/shard_map/ppermute | solution.py:114
  148.3 6.6 %collective-permute-start.18 = (bf16[2,64,512]{2,1,0:T(8,128)(2,1)S(1)}, bf16[2,64,512]{2,1,0:T(8,128)(2,1)S(1)}, u32[]{:S(2)}, u32[]{:S(2)}) collective-permute-start(bf16[2,64,512]{2,1,0:T(8,128)(2,1)S(1)} %fusion.67), channel_id=1, source_target_pairs={{0,1},{1,0},{2,3},{3,2},{4,5},{5,4},{6,7},{7,6},{8,9},{9,8},{10,11... | collective-permute-start | bytes 393224 | tf_op jit(solution)/shard_map/ppermute | solution.py:114
  155.0 10.9 %collective-permute-start.19 = (f32[2,32,512]{2,1,0:T(8,128)S(1)}, f32[2,32,512]{2,1,0:T(8,128)S(1)}, u32[]{:S(2)}, u32[]{:S(2)}) collective-permute-start(f32[2,32,512]{2,1,0:T(8,128)S(1)} %dynamic-slice_bitcast_fusion.3), channel_id=1, source_target_pairs={{0,1},{1,0},{2,3},{3,2},{4,5},{5,4},{6,7},{7,6},{8,9},{9,8},{10,11... | collective-permute-start | bytes 393224 | tf_op jit(solution)/shard_map/ppermute | solution.py:114
  156.7 6.6 %collective-permute-start.20 = (bf16[64,512]{1,0:T(8,128)(2,1)S(1)}, bf16[64,512]{1,0:T(8,128)(2,1)S(1)}, u32[]{:S(2)}, u32[]{:S(2)}) collective-permute-start(bf16[64,512]{1,0:T(8,128)(2,1)S(1)} %fusion.68), channel_id=1, source_target_pairs={{0,2},{1,3},{2,0},{3,1},{4,6},{5,7},{6,4},{7,5},{8,10},{9,11},{10,... | collective-permute-start | bytes 196616 | tf_op jit(solution)/shard_map/ppermute | solution.py:114
  159.3 6.6 %collective-permute-start.21 = (bf16[64,512]{1,0:T(8,128)(2,1)S(1)}, bf16[64,512]{1,0:T(8,128)(2,1)S(1)}, u32[]{:S(2)}, u32[]{:S(2)}) collective-permute-start(bf16[64,512]{1,0:T(8,128)(2,1)S(1)} %fusion.69), channel_id=1, source_target_pairs={{0,2},{1,3},{2,0},{3,1},{4,6},{5,7},{6,4},{7,5},{8,10},{9,11},{10,... | collective-permute-start | bytes 196616 | tf_op jit(solution)/shard_map/ppermute | solution.py:114
  182.3 6.4 %collective-permute-start.28 = (f32[128,512]{1,0:T(8,128)S(1)}, f32[128,512]{1,0:T(8,128)S(1)}, u32[]{:S(2)}, u32[]{:S(2)}) collective-permute-start(f32[128,512]{1,0:T(8,128)S(1)} %pad_maximum_fusion.5), channel_id=1, source_target_pairs={{0,16},{16,0},{1,17},{17,1},{2,18},{18,2},{3,19},{19,3},{4,20},{20... | collective-permute-start | bytes 786440 | tf_op jit(solution)/shard_map/ppermute | solution.py:114
  188.9 9.2 %collective-permute-start.30 = (f32[256,512]{1,0:T(8,128)S(1)}, f32[256,512]{1,0:T(8,128)S(1)}, u32[]{:S(2)}, u32[]{:S(2)}) collective-permute-start(f32[256,512]{1,0:T(8,128)S(1)} %pad_maximum_fusion.4), channel_id=1, source_target_pairs={{0,8},{4,12},{8,0},{12,4},{1,9},{5,13},{9,1},{13,5},{2,10},{6,14},... | collective-permute-start | bytes 1572872 | tf_op jit(solution)/shard_map/ppermute | solution.py:114
  (47 other events, 281.2 us)
